TPU v7x, 128 devices: a whole 4x4x4 slice. The times are simulated.
128 devices in a mesh: dp: 8 (over y, core), sp: 16 (over z, x).
Axes of the slice: x: 4, y: 4, z: 4, core: 2. Of those that a mesh axis runs over, the one named last changes fastest.
Arguments:
- queries: bfloat16 [8, 4096, 2048], P('dp', 'sp'), may hold values from -28 to 28
- keys: bfloat16 [8, 4096, 1024], P('dp', 'sp'), may hold values from -8 to 8
- values: bfloat16 [8, 4096, 1024], P('dp', 'sp'), may hold values from -6 to 6
- key_blocks: int32 [8, 16, 32, 8], P('dp', 'sp'), may hold values from 0 to 31, as said below
- block_counts: int32 [8, 16, 32], P('dp', 'sp'), may hold values from 1 to 8, as said below
- doc_lengths: int32 [8, 16], P('dp'), may hold values from 1 to 1024, 4096 in all within a row
- out_weight: bfloat16 [2048, 3072], P('sp'), may hold values from -0.125 to 0.125
- d_out: bfloat16 [8, 4096, 3072], P('dp', 'sp'), may hold values from -6 to 6
Outputs:
- layer_out: bfloat16 [8, 4096, 3072], P('dp', 'sp')
- grad_queries: bfloat16 [8, 4096, 2048], P('dp', 'sp')
- grad_keys: bfloat16 [8, 4096, 1024], P('dp', 'sp')
- grad_values: bfloat16 [8, 4096, 1024], P('dp', 'sp')
- grad_weight: float32 [2048, 3072], P('sp')
Inputs may be any that keep to these rules, and one draw needn't show every extreme that they name: `key_blocks`: entry 0 of the list of query block b names b; the first block_counts entries name distinct blocks, none after b; later entries name other blocks. `block_counts`: for query block b at most b + 1.
All inputs are finite; a program needn't handle non-finite values.
Results may differ from a plain program's by a relative error of at most 0.022.
Values may be sent and summed in bfloat16 or wider, within the bound.
A program may use at most 128 MiB of HBM per device.

v0:
```python
import math

import jax
import jax.numpy as jnp
from jax import lax
from jax.sharding import PartitionSpec as P

NEG_FILL = -jnp.inf


def doc_starts(lengths):
    return jnp.cumsum(lengths, dtype=jnp.int32) - lengths


def doc_of(positions, starts):
    return jnp.sum((positions[..., None] >= starts).astype(jnp.int32), axis=-1, dtype=jnp.int32) - 1


def group_mask(group_index, chosen, used, starts, width):
    blocks, slots = chosen.shape
    query_pos = (group_index * blocks + jnp.arange(blocks, dtype=jnp.int32))[:, None] * width
    query_pos = query_pos + jnp.arange(width, dtype=jnp.int32)[None, :]
    key_pos = chosen[:, :, None] * width + jnp.arange(width, dtype=jnp.int32)[None, None, :]
    key_pos = key_pos.reshape(blocks, slots * width)
    slot_ok = jnp.repeat(jnp.arange(slots, dtype=jnp.int32)[None, :] < used[:, None], width, axis=1)
    same_doc = doc_of(query_pos, starts)[:, :, None] == doc_of(key_pos, starts)[:, None, :]
    return slot_ok[:, None, :] & (key_pos[:, None, :] <= query_pos[:, :, None]) & same_doc


def selector_of(chosen, nblocks, dtype):
    flat = chosen.reshape(-1)
    return (flat[:, None] == jnp.arange(nblocks, dtype=jnp.int32)[None, :]).astype(dtype)


def gathered(table, chosen):
    blocks, slots = chosen.shape
    nblocks, width, size = table.shape
    selector = selector_of(chosen, nblocks, table.dtype)
    rows = jnp.dot(
        selector, table.reshape(nblocks, width * size), preferred_element_type=jnp.float32
    )
    return rows.astype(table.dtype).reshape(blocks, slots * width, size)


def add_into(total, chosen, parts):
    nblocks, width, size = total.shape
    selector = selector_of(chosen, nblocks, jnp.float32)
    flat_parts = parts.reshape(selector.shape[0], width * size)
    added = lax.dot_general(
        selector,
        flat_parts,
        (((0,), (0,)), ((), ())),
        precision=lax.Precision.HIGHEST,
        preferred_element_type=jnp.float32,
    )
    return total + added.reshape(nblocks, width, size)


def front_product(left, table, chosen):
    return jnp.einsum(
        "gqd,gkd->gqk", left, gathered(table, chosen), preferred_element_type=jnp.float32
    )


def back_product(weights, table, chosen):
    return jnp.einsum(
        "gqk,gkd->gqd", weights, gathered(table, chosen), preferred_element_type=jnp.float32
    )


def slot_product(weights, right):
    return jnp.einsum("gqk,gqd->gkd", weights, right, preferred_element_type=jnp.float32)


def attend(query_head, key_head, value_head, chosen_all, used_all, starts, scale):
    nblocks, slots = chosen_all.shape
    length, size = query_head.shape
    width = length // nblocks
    groups = nblocks // 4
    key_table = key_head.reshape(nblocks, width, size)
    value_table = value_head.reshape(nblocks, width, size)

    def one(inputs):
        query_group, chosen, used, index = inputs
        mask = group_mask(index, chosen, used, starts, width)
        scores = front_product(query_group, key_table, chosen) * scale
        scores = jnp.where(mask, scores, NEG_FILL)
        top = jnp.max(scores, axis=2)
        weights = jnp.where(mask, jnp.exp(scores - top[:, :, None]), 0.0)
        total = jnp.sum(weights, axis=2)
        probs = (weights / total[:, :, None]).astype(jnp.bfloat16)
        result = back_product(probs, value_table, chosen).astype(jnp.bfloat16)
        return (result, top + jnp.log(total))

    inputs = (
        query_head.reshape(groups, 4, width, size),
        chosen_all.reshape(groups, 4, slots),
        used_all.reshape(groups, 4),
        jnp.arange(groups, dtype=jnp.int32),
    )
    results, log_total = lax.map(one, inputs)
    return (results.reshape(length, size), log_total.reshape(length))


def attend_back(
    query_head,
    key_head,
    value_head,
    attn_head,
    grad_head,
    log_total,
    chosen_all,
    used_all,
    starts,
    scale,
):
    nblocks, slots = chosen_all.shape
    length, size = query_head.shape
    width = length // nblocks
    groups = nblocks // 4
    key_table = key_head.reshape(nblocks, width, size)
    value_table = value_head.reshape(nblocks, width, size)

    def step(carry, inputs):
        sum_keys, sum_values = carry
        query_group, attn_group, grad_group, total_group, chosen, used, index = inputs
        mask = group_mask(index, chosen, used, starts, width)
        scores = front_product(query_group, key_table, chosen) * scale
        scores = jnp.where(mask, scores, NEG_FILL)
        back_probs = jnp.where(mask, jnp.exp(scores - total_group[:, :, None]), 0.0)
        back_round = back_probs.astype(jnp.bfloat16)
        delta = jnp.sum(grad_group.astype(jnp.float32) * attn_group.astype(jnp.float32), axis=2)
        grad_p = front_product(grad_group, value_table, chosen)
        grad_scores = (back_probs * (grad_p - delta[:, :, None])).astype(jnp.bfloat16)
        grad_query = back_product(grad_scores, key_table, chosen) * scale
        part_keys = slot_product(grad_scores, query_group)
        part_values = slot_product(back_round, grad_group)
        return (
            (add_into(sum_keys, chosen, part_keys), add_into(sum_values, chosen, part_values)),
            grad_query,
        )

    inputs = (
        query_head.reshape(groups, 4, width, size),
        attn_head.reshape(groups, 4, width, size),
        grad_head.reshape(groups, 4, width, size),
        log_total.reshape(groups, 4, width),
        chosen_all.reshape(groups, 4, slots),
        used_all.reshape(groups, 4),
        jnp.arange(groups, dtype=jnp.int32),
    )
    start = (
        jnp.zeros((nblocks, width, size), jnp.float32),
        jnp.zeros((nblocks, width, size), jnp.float32),
    )
    (sum_keys, sum_values), grad_query = lax.scan(step, start, inputs)
    return (
        grad_query.reshape(length, size),
        sum_keys.reshape(length, size) * scale,
        sum_values.reshape(length, size),
    )


def per_device(queries, keys, values, key_blocks, block_counts, doc_lengths, out_weight, d_out):
    query_tok = queries[0]
    key_tok = keys[0]
    value_tok = values[0]
    grad_out = d_out[0]
    chosen_all = key_blocks[0, 0]
    used_all = block_counts[0, 0]
    tokens, query_width = query_tok.shape
    seq_devices = lax.axis_size("sp")
    size = query_width // seq_devices
    kv_width = key_tok.shape[1]
    head_group = query_width // kv_width
    length = tokens * seq_devices
    scale = 1.0 / math.sqrt(size)
    starts = doc_starts(doc_lengths[0])
    wide_keys = jnp.repeat(
        key_tok.reshape(tokens, kv_width // size, size), head_group, axis=1
    ).reshape(tokens, query_width)
    wide_values = jnp.repeat(
        value_tok.reshape(tokens, kv_width // size, size), head_group, axis=1
    ).reshape(tokens, query_width)
    query_head, key_head, value_head = (
        lax.all_to_all(query_tok, "sp", split_axis=1, concat_axis=0, tiled=True),
        lax.all_to_all(wide_keys, "sp", split_axis=1, concat_axis=0, tiled=True),
        lax.all_to_all(wide_values, "sp", split_axis=1, concat_axis=0, tiled=True),
    )
    attn_head, log_total = attend(
        query_head, key_head, value_head, chosen_all, used_all, starts, scale
    )
    attn_tok = lax.all_to_all(attn_head, "sp", split_axis=0, concat_axis=1, tiled=True)
    piece = lax.all_gather(out_weight, "sp", axis=0, tiled=True)
    columns = attn_tok
    out_sum = jnp.dot(columns, piece, preferred_element_type=jnp.float32)
    grad_part = lax.dot_general(
        grad_out, piece, (((1,), (1,)), ((), ())), preferred_element_type=jnp.float32
    )
    layer_out = out_sum.astype(jnp.bfloat16)
    grad_head = lax.all_to_all(
        grad_part.astype(jnp.bfloat16), "sp", split_axis=1, concat_axis=0, tiled=True
    )
    grad_query, grad_key, grad_value = attend_back(
        query_head,
        key_head,
        value_head,
        attn_head,
        grad_head,
        log_total,
        chosen_all,
        used_all,
        starts,
        scale,
    )
    wide_q, wide_k, wide_v = (
        lax.all_to_all(
            grad_query.astype(jnp.bfloat16), "sp", split_axis=0, concat_axis=1, tiled=True
        ).astype(grad_query.dtype),
        lax.all_to_all(
            grad_key.astype(jnp.bfloat16), "sp", split_axis=0, concat_axis=1, tiled=True
        ).astype(grad_key.dtype),
        lax.all_to_all(
            grad_value.astype(jnp.bfloat16), "sp", split_axis=0, concat_axis=1, tiled=True
        ).astype(grad_value.dtype),
    )
    grad_q_tok = wide_q.astype(jnp.bfloat16)
    grad_k_tok = jnp.sum(
        wide_k.reshape(tokens, kv_width // size, head_group, size), axis=2
    ).reshape(tokens, kv_width)
    grad_k_tok = grad_k_tok.astype(jnp.bfloat16)
    grad_v_tok = jnp.sum(
        wide_v.reshape(tokens, kv_width // size, head_group, size), axis=2
    ).reshape(tokens, kv_width)
    grad_v_tok = grad_v_tok.astype(jnp.bfloat16)
    columns = attn_tok
    shard_rows = lax.psum_scatter(
        lax.dot_general(
            columns, grad_out, (((0,), (0,)), ((), ())), preferred_element_type=jnp.float32
        ).astype(jnp.bfloat16),
        "sp",
        scatter_dimension=0,
        tiled=True,
    )
    summed = lax.psum(shard_rows, "dp").astype(jnp.float32)
    grad_weight = summed * (1.0 / math.sqrt(lax.axis_size("dp") * length))
    return (layer_out[None], grad_q_tok[None], grad_k_tok[None], grad_v_tok[None], grad_weight)


def solution(mesh):
    in_specs = (
        P("dp", "sp", None),
        P("dp", "sp", None),
        P("dp", "sp", None),
        P("dp", "sp", None, None),
        P("dp", "sp", None),
        P("dp", None),
        P("sp", None),
        P("dp", "sp", None),
    )
    out_specs = (
        P("dp", "sp", None),
        P("dp", "sp", None),
        P("dp", "sp", None),
        P("dp", "sp", None),
        P("sp", None),
    )
    return jax.shard_map(
        per_device, mesh=mesh, in_specs=in_specs, out_specs=out_specs, check_vma=False
    )
```

profile of v0, /device:TPU:1, one launch (start us, length us, event | category | flops | bytes accessed | tf_op | source)
XLA Modules:
  0.0 566.0 jit_solution(1316093496710761916)
XLA Ops:
  9.7 8.4 %all-to-all-start.1 = ((bf16[256,16,128]{2,0,1:T(8,128)(2,1)}), bf16[256,16,128]{2,0,1:T(8,128)(2,1)S(1)}, u32[]{:S(2)}, u32[]{:S(2)}) async-start(bf16[256,16,128]{2,0,1:T(8,128)(2,1)} %bitcast.299), calls=%async_computation.1 | async-start | bytes 2097152 | tf_op jit(solution)/shard_map/all_to_all | solution.py:187
  18.3 15.8 %all-to-all-done.1 = bf16[256,16,128]{2,0,1:T(8,128)(2,1)S(1)} async-done(((bf16[256,16,128]{2,0,1:T(8,128)(2,1)}), bf16[256,16,128]{2,0,1:T(8,128)(2,1)S(1)}, u32[]{:S(2)}, u32[]{:S(2)}) %all-to-all-start.1) | async-done | bytes 1048608 | tf_op jit(solution)/shard_map/all_to_all | solution.py:187
  35.4 4.4 all-to-all-start.2
  42.5 12.1 %all-to-all-done.2 = bf16[256,16,128]{2,0,1:T(8,128)(2,1)} async-done(((bf16[256,16,128]{2,0,1:T(8,128)(2,1)}), bf16[256,16,128]{2,0,1:T(8,128)(2,1)}, u32[]{:S(2)}, u32[]{:S(2)}) %all-to-all-start.2) | async-done | bytes 1048608 | tf_op jit(solution)/shard_map/all_to_all | solution.py:188
  54.6 4.3 all-to-all-start
  64.9 7.8 %all-to-all-done = bf16[256,16,128]{2,0,1:T(8,128)(2,1)} async-done(((bf16[256,16,128]{2,0,1:T(8,128)(2,1)}), bf16[256,16,128]{2,0,1:T(8,128)(2,1)}, u32[]{:S(2)}, u32[]{:S(2)}) %all-to-all-start) | async-done | bytes 1048608 | tf_op jit(solution)/shard_map/all_to_all | solution.py:186
  72.7 108.6 %while.35 = (s32[]{:T(128)}, bf16[8,4,128,128]{3,2,1,0:T(8,128)(2,1)}, f32[8,4,128]{2,1,0:T(4,128)S(1)}, s32[8,4]{1,0:T(8,128)S(1)}, s32[8,4,8]{2,1,0:T(4,128)S(...) while((s32[]{:T(128)}, ...), condition=%wide.wide.region_6.7_spmd, body=%wide.wide.region_1.6_spmd.sunk | while | flops 350517312 | bytes 21519848 | solution.py:101
  181.3 4.3 all-to-all-start.3
  189.5 9.6 %all-to-all-done.3 = bf16[16,256,128]{2,1,0:T(8,128)(2,1)} async-done(((bf16[16,256,128]{2,1,0:T(8,128)(2,1)}), bf16[16,256,128]{2,1,0:T(8,128)(2,1)}, u32[]{:S(2)}, u32[]{:S(2)}) %all-to-all-start.3) | async-done | bytes 1048608 | tf_op jit(solution)/shard_map/all_to_all | solution.py:193
  201.3 6.6 %fusion.54 = bf16[32,16,8,128]{3,2,1,0:T(8,128)(2,1)S(1)} fusion(bf16[2048,3072]{1,0:T(8,128)(2,1)} %all-gather.2.cloned.1.call-done, bf16[1,256,3072]{2,1,0:T(8,128)(2,1)S(1)} %copy-done), kind=kOutput, calls=%fused_computation.103 | convolution fusion | flops 3221749760 | bytes 15204352 | tf_op jit(solution)/shard_map/dot_general | solution.py:197
  209.1 4.3 all-to-all-start.4
  213.7 7.6 %convolution_convert_fusion.5 = bf16[2048,3072]{1,0:T(8,128)(2,1)} fusion(bf16[256,2048]{0,1:T(8,128)(2,1)} %bitcast.294, bf16[1,256,3072]{2,1,0:T(8,128)(2,1)S(1)} %copy-done), kind=kOutput, calls=%fused_computation.93 | convolution fusion | flops 3227516928 | bytes 15204352 | tf_op jit(solution)/shard_map/dot_general | solution.py:238
  221.3 4.5 all-to-all-done.4
  225.8 238.6 %while.36 = (s32[]{:T(128)}, f32[32,128,128]{2,0,1:T(8,128)}, f32[32,128,128]{2,0,1:T(8,128)}, bf16[8,4,128,128]{3,2,1,0:T(8,128)(2,1)}, s32[8,4,8]{2,1,0:T(4,12...) while((s32[]{:T(128)}, f32[32,128,128]{2,0,1:T(8,128)}, ...), condition=%wide.wide.region_11.12_spmd.clone, body=%wide.wide.region_7.11_spmd.clone.sunk | while | flops 1150844928 | bytes 68355992 | solution.py:156
  235.6 2.8 fusion.164
  241.1 4.1 select_add_fusion.6
  245.2 2.8 fusion.165
  263.5 2.8 fusion.164
  266.2 2.9 reshape.453
  269.1 4.8 select_add_fusion.6
  273.9 2.8 fusion.165
  278.4 4.4 select_add_fusion.7
  293.9 2.8 fusion.164
  299.5 4.7 select_add_fusion.6
  304.2 2.8 fusion.165
  308.8 4.3 select_add_fusion.7
  329.5 4.7 select_add_fusion.6
  334.3 2.8 fusion.165
  338.8 4.2 select_add_fusion.7
  359.6 4.7 select_add_fusion.6
  364.3 2.8 fusion.165
  368.9 4.2 select_add_fusion.7
  389.6 4.7 select_add_fusion.6
  394.3 2.8 fusion.165
  398.9 4.2 select_add_fusion.7
  419.6 4.7 select_add_fusion.6
  424.4 2.8 fusion.165
  428.9 4.2 select_add_fusion.7
  449.7 4.7 select_add_fusion.6
  454.4 2.8 fusion.165
  458.9 4.2 select_add_fusion.7
  464.4 4.5 all-to-all-start.5
  471.3 10.3 %all-to-all-done.5 = bf16[16,256,128]{2,1,0:T(8,128)(2,1)S(1)} async-done(((bf16[16,256,128]{2,1,0:T(8,128)(2,1)}), bf16[16,256,128]{2,1,0:T(8,128)(2,1)S(1)}, u32[]{:S(2)}, u32[]{:S(2)}) %all-to-all-start.5) | async-done | bytes 1048608 | tf_op jit(solution)/shard_map/all_to_all | solution.py:217
  481.5 4.3 all-to-all-start.6
  488.3 9.8 %all-to-all-done.6 = bf16[16,256,128]{2,1,0:T(8,128)(2,1)} async-done(((bf16[16,256,128]{2,1,0:T(8,128)(2,1)}), bf16[16,256,128]{2,1,0:T(8,128)(2,1)}, u32[]{:S(2)}, u32[]{:S(2)}) %all-to-all-start.6) | async-done | bytes 1048608 | tf_op jit(solution)/shard_map/all_to_all | solution.py:220
  498.2 4.3 all-to-all-start.7
  502.5 9.2 %fusion.50 = bf16[1,256,3072]{2,1,0:T(8,128)(2,1)} fusion(bf16[256,2048]{0,1:T(8,128)(2,1)S(1)} %bitcast.295, bf16[2048,3072]{1,0:T(8,128)(2,1)} %all-gather.2.cloned.1.call-done), kind=kOutput, calls=%fused_computation.95 | convolution fusion | flops 3222011904 | bytes 15204352 | tf_op jit(solution)/shard_map/dot_general | solution.py:196
  519.1 37.9 %all-reduce.2.cloned.1.call-done = bf16[128,3072]{1,0:T(8,128)(2,1)} async-done(((bf16[128,3072]{1,0:T(8,128)(2,1)}), bf16[128,3072]{1,0:T(8,128)(2,1)}) %all-reduce.2.cloned.1.call-update) | async-done | bytes 786448 | tf_op jit(solution)/shard_map/psum | solution.py:245
  (578 shorter events, 269.6 us)
Async XLA Ops:
  7.2 194.2 %copy-start = (bf16[1,256,3072]{2,1,0:T(8,128)(2,1)S(1)}, bf16[1,256,3072]{2,1,0:T(8,128)(2,1)}, u32[]{:S(2)}) copy-start(bf16[1,256,3072]{2,1,0:T(8,128)(2,1)} %param.19) | copy-start | bytes 4718596
  8.5 9.6 %copy-start.12 = (bf16[1,256,1024]{2,1,0:T(8,128)(2,1)S(1)}, bf16[1,256,1024]{2,1,0:T(8,128)(2,1)}, u32[]{:S(2)}) copy-start(bf16[1,256,1024]{2,1,0:T(8,128)(2,1)} %param.14) | copy-start | bytes 1572868
  9.7 24.4 %all-to-all-start.1 = ((bf16[256,16,128]{2,0,1:T(8,128)(2,1)}), bf16[256,16,128]{2,0,1:T(8,128)(2,1)S(1)}, u32[]{:S(2)}, u32[]{:S(2)}) async-start(bf16[256,16,128]{2,0,1:T(8,128)(2,1)} %bitcast.299), calls=%async_computation.1 | async-start | bytes 2097152 | tf_op jit(solution)/shard_map/all_to_all | solution.py:187
  34.1 29.6 %copy-start.11 = (bf16[256,16,128]{2,0,1:T(8,128)(2,1)}, bf16[256,16,128]{2,0,1:T(8,128)(2,1)S(1)}, u32[]{:S(2)}) copy-start(bf16[256,16,128]{2,0,1:T(8,128)(2,1)S(1)} %all-to-all-done.1) | copy-start | bytes 3145732
  35.4 19.2 %all-to-all-start.2 = ((bf16[256,16,128]{2,0,1:T(8,128)(2,1)}), bf16[256,16,128]{2,0,1:T(8,128)(2,1)}, u32[]{:S(2)}, u32[]{:S(2)}) async-start(bf16[256,16,128]{2,0,1:T(8,128)(2,1)} %bitcast.300), calls=%async_computation.2 | async-start | bytes 2097152 | tf_op jit(solution)/shard_map/all_to_all | solution.py:188
  41.3 19.0 %copy-start.15 = (s32[1,1,32]{2,1,0:T(1,128)S(1)}, s32[1,1,32]{2,1,0:T(1,128)}, u32[]{:S(2)}) copy-start(s32[1,1,32]{2,1,0:T(1,128)} %param.16) | copy-start | bytes 388
  41.3 19.7 %copy-start.13 = (s32[1,1,32,8]{2,3,1,0:T(8,128)S(1)}, s32[1,1,32,8]{2,3,1,0:T(8,128)}, u32[]{:S(2)}) copy-start(s32[1,1,32,8]{2,3,1,0:T(8,128)} %param.15) | copy-start | bytes 3076
  41.3 19.8 %copy-start.14 = (s32[1,16]{1,0:T(1,128)S(1)}, s32[1,16]{1,0:T(1,128)}, u32[]{:S(2)}) copy-start(s32[1,16]{1,0:T(1,128)} %param.17) | copy-start | bytes 196
  54.6 18.1 %all-to-all-start = ((bf16[256,16,128]{2,0,1:T(8,128)(2,1)}), bf16[256,16,128]{2,0,1:T(8,128)(2,1)}, u32[]{:S(2)}, u32[]{:S(2)}) async-start(bf16[256,16,128]{2,0,1:T(8,128)(2,1)} %copy.87), calls=%async_computation | async-start | bytes 2097152 | tf_op jit(solution)/shard_map/all_to_all | solution.py:186
  59.0 142.3 %all-gather.2.cloned.1.call-start = ((), (), s32[]{:S(2)}) async-start(), calls=%async_computation.9 | async-start | bytes 13369344 | tf_op jit(solution)/shard_map/all_gather | solution.py:194
  123.8 1.3 copy-start.9
  137.4 1.3 copy-start.9
  181.3 17.8 %all-to-all-start.3 = ((bf16[16,256,128]{2,1,0:T(8,128)(2,1)}), bf16[16,256,128]{2,1,0:T(8,128)(2,1)}, u32[]{:S(2)}, u32[]{:S(2)}) async-start(bf16[16,256,128]{2,1,0:T(8,128)(2,1)} %bitcast.303), calls=%async_computation.3 | async-start | bytes 2097152 | tf_op jit(solution)/shard_map/all_to_all | solution.py:193
  209.1 16.6 %all-to-all-start.4 = ((bf16[256,16,128]{2,0,1:T(8,128)(2,1)}), bf16[256,16,128]{2,0,1:T(8,128)(2,1)}, u32[]{:S(2)}, u32[]{:S(2)}) async-start(bf16[256,16,128]{2,0,1:T(8,128)(2,1)} %bitcast.298), calls=%async_computation.4 | async-start | bytes 2097152 | tf_op jit(solution)/shard_map/all_to_all | solution.py:201
  213.5 274.8 %reduce-scatter.2.cloned.1.call-start = ((), (), s32[]{:S(2)}) async-start(), calls=%async_computation.10 | async-start | bytes 13369344 | tf_op jit(solution)/shard_map/reduce_scatter | solution.py:237
  226.9 3.9 copy-start.2
  228.8 2.1 copy-start.8
  249.8 2.5 copy-start.3
  252.3 1.3 copy-start.7
  254.8 3.9 copy-start.2
  256.6 2.1 copy-start.8
  278.4 4.5 copy-start.3
  285.3 3.9 copy-start.2
  287.1 2.1 copy-start.8
  308.7 4.3 copy-start.3
  315.4 3.9 copy-start.2
  317.2 2.1 copy-start.8
  338.8 4.2 copy-start.3
  345.4 3.9 copy-start.2
  347.3 2.1 copy-start.8
  368.8 4.2 copy-start.3
  375.4 3.9 copy-start.2
  377.3 2.1 copy-start.8
  398.9 4.2 copy-start.3
  405.4 3.9 copy-start.2
  407.3 2.1 copy-start.8
  428.9 4.2 copy-start.3
  435.5 3.9 copy-start.2
  437.3 2.1 copy-start.8
  458.9 4.2 copy-start.3
  464.4 4.6 copy-start.4
  464.4 17.1 %all-to-all-start.5 = ((bf16[16,256,128]{2,1,0:T(8,128)(2,1)}), bf16[16,256,128]{2,1,0:T(8,128)(2,1)S(1)}, u32[]{:S(2)}, u32[]{:S(2)}) async-start(bf16[16,256,128]{2,1,0:T(8,128)(2,1)} %bitcast.309), calls=%async_computation.5 | async-start | bytes 2097152 | tf_op jit(solution)/shard_map/all_to_all | solution.py:217
  471.3 14.9 %copy-start.5 = (f32[32,128,128]{2,0,1:T(8,128)S(1)}, f32[32,128,128]{2,0,1:T(8,128)}, u32[]{:S(2)}) copy-start(f32[32,128,128]{2,0,1:T(8,128)} %get-tuple-element.370) | copy-start | bytes 6291460
  481.5 16.7 %all-to-all-start.6 = ((bf16[16,256,128]{2,1,0:T(8,128)(2,1)}), bf16[16,256,128]{2,1,0:T(8,128)(2,1)}, u32[]{:S(2)}, u32[]{:S(2)}) async-start(bf16[16,256,128]{2,1,0:T(8,128)(2,1)} %bitcast.31), calls=%async_computation.6 | async-start | bytes 2097152 | tf_op jit(solution)/shard_map/all_to_all | solution.py:220
  485.9 71.1 %all-reduce.2.cloned.1.call-start = ((), (), s32[]{:S(2)}) async-start(), calls=%async_computation.11 | async-start | bytes 1572864 | tf_op jit(solution)/shard_map/psum | solution.py:245
  488.3 14.2 %copy-start.10 = (bf16[256,16,128]{0,2,1:T(8,128)(2,1)S(1)}, bf16[256,16,128]{0,2,1:T(8,128)(2,1)}, u32[]{:S(2)}) copy-start(bf16[256,16,128]{0,2,1:T(8,128)(2,1)} %copy.90) | copy-start | bytes 3145732
  498.2 18.2 %all-to-all-start.7 = ((bf16[16,256,128]{2,1,0:T(8,128)(2,1)}), bf16[16,256,128]{2,1,0:T(8,128)(2,1)}, u32[]{:S(2)}, u32[]{:S(2)}) async-start(bf16[16,256,128]{2,1,0:T(8,128)(2,1)} %bitcast.35), calls=%async_computation.7 | async-start | bytes 2097152 | tf_op jit(solution)/shard_map/all_to_all | solution.py:223
  516.4 43.1 %copy-start.1 = (bf16[1,256,3072]{2,1,0:T(8,128)(2,1)S(1)}, bf16[1,256,3072]{2,1,0:T(8,128)(2,1)}, u32[]{:S(2)}) copy-start(bf16[1,256,3072]{2,1,0:T(8,128)(2,1)} %param.19) | copy-start | bytes 4718596
  (21 other events, 25.0 us)
Sparse Core Ops, SparseCore 0:
  62.0 94.7 all-gather.1
  221.5 100.6 reduce-scatter.1
  489.1 67.8 all-reduce.1
where the time goes:
time: 571 us; the launch traced here: 566 us
  matrix products  246 us (43%)
  local copies, waits for them, and re-layouts  113 us (20%)
  waiting for transfers between devices  108 us (19%)
  starting transfers between devices  39.5 us (7%)
  other arithmetic  33.1 us (6%)
  between operations  14 us (2%)
  loops' own time  11.8 us (2%)
    dot_general x16, matrix products, add_into(): lax.dot_general(selector, flat_parts, (((0,), (0,)), ((), ())), precision...  69.6 us
    dot_general x24, matrix products, front_product(): jnp.einsum('gqd,gkd->gqk', left, gathered(table, chosen), preferred_eleme...  48.5 us
    dot_general x16, matrix products, slot_product(): jnp.einsum('gqk,gqd->gkd', weights, right, preferred_element_type=jnp.flo...  44.3 us
    psum x1, waiting for transfers between devices, per_device(): summed = lax.psum(shard_rows, 'dp').astype(jnp.float32)  37.9 us
    reshape x16, local copies, waits for them, and re-layouts, add_into(): flat_parts = parts.reshape(selector.shape[0], width * size)  36.2 us
    reshape x32, local copies, waits for them, and re-layouts, gathered(): return rows.astype(table.dtype).reshape(blocks, slots * width, size)  36.1 us
    dot_general x32, matrix products, gathered(): jnp.dot(selector, table.reshape(nblocks, width * size), preferred_element...  35.3 us
    dot_general x16, matrix products, back_product(): jnp.einsum('gqk,gkd->gqd', weights, gathered(table, chosen), preferred_el...  25.3 us
  transfers between devices with their start and end apart: 11, of which 8 were waited for; matrix products, arithmetic and copies ran while one was open for 66% of the time, Pallas kernels for 0%

commit v1 on v0

v1 whole, which is shorter than its diff:
```python
import math

import jax
import jax.numpy as jnp
from jax import lax
from jax.experimental import pallas as pl
from jax.experimental.pallas import tpu as pltpu
from jax.sharding import PartitionSpec as P

SIZE = 128
TOK = 256
HALO = 4
BAND = (HALO + 1) * TOK
KB = BAND // SIZE
NEG = -1e30
BF = jnp.bfloat16
F32 = jnp.float32
NT = (((1,), (1,)), ((), ()))
TN = (((0,), (0,)), ((), ()))


def forward_body(q_ref, k_ref, v_ref, list_ref, bias_ref, attn_t_ref, attn_ref, p_ref, r_ref):
    scale = 1.0 / math.sqrt(SIZE)
    factor = scale * math.log2(math.e)
    for h in range(2):
        lanes = slice(h * SIZE, (h + 1) * SIZE)
        q = q_ref[:, lanes]
        tops = []
        scores = []
        for b in range(KB):
            rows = slice(b * SIZE, (b + 1) * SIZE)
            s = lax.dot_general(k_ref[rows, :], q, NT, preferred_element_type=F32)
            s = s + bias_ref[rows, :] + list_ref[h, b : b + 1, :]
            scores.append(s)
            tops.append(jnp.max(s, axis=0, keepdims=True))
        top = tops[0]
        for t in tops[1:]:
            top = jnp.maximum(top, t)
        total = jnp.zeros((1, TOK), F32)
        out = jnp.zeros((SIZE, TOK), F32)
        for b in range(KB):
            rows = slice(b * SIZE, (b + 1) * SIZE)
            p = jnp.exp2((scores[b] - top) * factor)
            total = total + jnp.sum(p, axis=0, keepdims=True)
            p_ref[h, rows, :] = p.astype(BF)
        out = lax.dot_general(v_ref[...], p_ref[h], TN, preferred_element_type=F32)
        inverse = 1.0 / total
        r_ref[h] = jnp.broadcast_to(inverse, (8, TOK))
        out = out * inverse
        attn_t_ref[lanes, :] = out.astype(BF)
        attn_ref[:, lanes] = out.T.astype(BF)


def forward_kernel(q_ref, k_ref, v_ref, list_ref, dq_ref, dk_ref, attn_t_ref, attn_ref, p_ref, r_ref, bias_ref):
    @pl.when(pl.program_id(0) == 0)
    def _():
        same = dk_ref[:, 0:1] == dq_ref[0:1, :]
        causal = dk_ref[:, 1:2] <= dq_ref[1:2, :]
        bias_ref[...] = jnp.where(same & causal, 0.0, NEG)

    forward_body(q_ref, k_ref, v_ref, list_ref, bias_ref, attn_t_ref, attn_ref, p_ref, r_ref)


def backward_kernel(q_ref, k_ref, v_ref, p_ref, r_ref, attn_t_ref, g_t_ref, dq_ref, dk_ref, dv_ref):
    scale = 1.0 / math.sqrt(SIZE)
    dk = jnp.zeros((BAND, SIZE), F32)
    dv = jnp.zeros((BAND, SIZE), F32)
    for h in range(2):
        lanes = slice(h * SIZE, (h + 1) * SIZE)
        inverse = r_ref[h, 0:1, :]
        g_t = g_t_ref[lanes, :].astype(F32)
        delta = jnp.sum(g_t * attn_t_ref[lanes, :].astype(F32), axis=0, keepdims=True) * inverse
        g_t = g_t * inverse
        g = g_t.T.astype(BF)
        dp = jnp.dot(v_ref[...], g_t.astype(BF), preferred_element_type=F32)
        p = p_ref[h]
        ds = (p.astype(F32) * (dp - delta)).astype(BF)
        dq_t = lax.dot_general(k_ref[...], ds, TN, preferred_element_type=F32)
        dq_ref[:, lanes] = (dq_t * scale).T.astype(BF)
        dk = dk + jnp.dot(ds, q_ref[:, lanes], preferred_element_type=F32)
        dv = dv + jnp.dot(p, g, preferred_element_type=F32)
    dk_ref[...] = (dk * scale).astype(BF)
    dv_ref[...] = dv.astype(BF)


def call_forward(q, k, v, lists, dq, dk):
    return pl.pallas_call(
        forward_kernel,
        grid=(8,),
        in_specs=[
            pl.BlockSpec((TOK, 2 * SIZE), lambda c: (0, c)),
            pl.BlockSpec((BAND, SIZE), lambda c: (0, c)),
            pl.BlockSpec((BAND, SIZE), lambda c: (0, c)),
            pl.BlockSpec((2, 16, TOK), lambda c: (c, 0, 0)),
            pl.BlockSpec((8, TOK), lambda c: (0, 0)),
            pl.BlockSpec((BAND, 2), lambda c: (0, 0)),
        ],
        out_specs=[
            pl.BlockSpec((2 * SIZE, TOK), lambda c: (c, 0)),
            pl.BlockSpec((TOK, 2 * SIZE), lambda c: (0, c)),
            pl.BlockSpec((2, BAND, TOK), lambda c: (c, 0, 0)),
            pl.BlockSpec((2, 8, TOK), lambda c: (c, 0, 0)),
        ],
        out_shape=[
            jax.ShapeDtypeStruct((2048, TOK), BF),
            jax.ShapeDtypeStruct((TOK, 2048), BF),
            jax.ShapeDtypeStruct((16, BAND, TOK), BF),
            jax.ShapeDtypeStruct((16, 8, TOK), F32),
        ],
        scratch_shapes=[pltpu.VMEM((BAND, TOK), F32)],
        compiler_params=pltpu.CompilerParams(vmem_limit_bytes=32 * 2**20),
        cost_estimate=pl.CostEstimate(flops=6 * 10**9, bytes_accessed=20 * 10**6, transcendentals=6 * 10**6),
    )(q, k, v, lists, dq, dk)


def call_backward(q, k, v, p, r, attn_t, g_t):
    return pl.pallas_call(
        backward_kernel,
        grid=(8,),
        in_specs=[
            pl.BlockSpec((TOK, 2 * SIZE), lambda c: (0, c)),
            pl.BlockSpec((BAND, SIZE), lambda c: (0, c)),
            pl.BlockSpec((BAND, SIZE), lambda c: (0, c)),
            pl.BlockSpec((2, BAND, TOK), lambda c: (c, 0, 0)),
            pl.BlockSpec((2, 8, TOK), lambda c: (c, 0, 0)),
            pl.BlockSpec((2 * SIZE, TOK), lambda c: (c, 0)),
            pl.BlockSpec((2 * SIZE, TOK), lambda c: (c, 0)),
        ],
        out_specs=[
            pl.BlockSpec((TOK, 2 * SIZE), lambda c: (0, c)),
            pl.BlockSpec((BAND, SIZE), lambda c: (0, c)),
            pl.BlockSpec((BAND, SIZE), lambda c: (0, c)),
        ],
        out_shape=[
            jax.ShapeDtypeStruct((TOK, 2048), BF),
            jax.ShapeDtypeStruct((BAND, 1024), BF),
            jax.ShapeDtypeStruct((BAND, 1024), BF),
        ],
        compiler_params=pltpu.CompilerParams(vmem_limit_bytes=32 * 2**20),
        cost_estimate=pl.CostEstimate(flops=10 * 10**9, bytes_accessed=30 * 10**6, transcendentals=0),
    )(q, k, v, p, r, attn_t, g_t)


def documents(positions, lengths):
    starts = jnp.cumsum(lengths, dtype=jnp.int32) - lengths
    return jnp.sum((positions[:, None] >= starts[None, :]).astype(jnp.int32), axis=1, dtype=jnp.int32) - 1


def list_terms(key_blocks, block_counts):
    slots = jnp.arange(8, dtype=jnp.int32)
    used = slots[None, :] < block_counts[:, None]
    device = jnp.arange(32, dtype=jnp.int32) // 2
    band = 2 * device[:, None] - 2 * HALO + jnp.arange(16, dtype=jnp.int32)[None, :]
    listed = jnp.any((key_blocks[:, None, :] == band[:, :, None]) & used[:, None, :], axis=2)
    term = jnp.where(listed, 0.0, NEG).astype(F32).reshape(16, 2, 16).transpose(0, 2, 1)
    return jnp.repeat(term, SIZE, axis=2)


def per_device(queries, keys, values, key_blocks, block_counts, doc_lengths, out_weight, d_out):
    q = queries[0]
    grad_out = d_out[0]
    me = lax.axis_index("sp")
    n = lax.axis_size("sp")
    piece = lax.all_gather(out_weight, "sp", axis=0, tiled=True)
    lists = lax.all_to_all(list_terms(key_blocks[0, 0], block_counts[0, 0]), "sp", split_axis=0, concat_axis=0, tiled=True)
    kv = jnp.concatenate([keys[0], values[0]], axis=1)
    parts = [lax.ppermute(kv, "sp", [(i, (i + s) % n) for i in range(n)]) for s in range(HALO, 0, -1)]
    band = jnp.concatenate(parts + [kv], axis=0)
    k, v = band[:, :1024], band[:, 1024:]
    q_pos = me * TOK + jnp.arange(TOK, dtype=jnp.int32)
    k_pos = (me - HALO) * TOK + jnp.arange(BAND, dtype=jnp.int32)
    dq = jnp.zeros((8, TOK), jnp.int32).at[0].set(documents(q_pos, doc_lengths[0])).at[1].set(q_pos)
    dk = jnp.stack([documents(k_pos, doc_lengths[0]), k_pos], axis=1)
    attn_t, attn, p, r = call_forward(q, k, v, lists, dq, dk)
    layer_out = jnp.dot(attn, piece, preferred_element_type=F32).astype(BF)
    g_t = lax.dot_general(piece, grad_out, NT, preferred_element_type=F32).astype(BF)
    weight_part = jnp.dot(attn_t, grad_out, preferred_element_type=F32).astype(BF)
    shard_rows = lax.psum_scatter(weight_part, "sp", scatter_dimension=0, tiled=True)
    summed = lax.psum(shard_rows, "dp").astype(F32)
    grad_weight = summed * (1.0 / math.sqrt(lax.axis_size("dp") * n * TOK))
    grad_q, dk_band, dv_band = call_backward(q, k, v, p, r, attn_t, g_t)
    dkv = jnp.concatenate([dk_band, dv_band], axis=1)
    total = dkv[HALO * TOK :].astype(F32)
    for s in range(HALO, 0, -1):
        piece_back = dkv[(HALO - s) * TOK : (HALO - s + 1) * TOK]
        back = lax.ppermute(piece_back, "sp", [(i, (i - s) % n) for i in range(n)])
        total = total + back.astype(F32)
    total = total.astype(BF)
    return (layer_out[None], grad_q[None], total[None, :, :1024], total[None, :, 1024:], grad_weight)


def solution(mesh):
    in_specs = (
        P("dp", "sp", None),
        P("dp", "sp", None),
        P("dp", "sp", None),
        P("dp", "sp", None, None),
        P("dp", "sp", None),
        P("dp", None),
        P("sp", None),
        P("dp", "sp", None),
    )
    out_specs = (
        P("dp", "sp", None),
        P("dp", "sp", None),
        P("dp", "sp", None),
        P("dp", "sp", None),
        P("sp", None),
    )
    return jax.shard_map(per_device, mesh=mesh, in_specs=in_specs, out_specs=out_specs, check_vma=False)
```

time: 571 us -> 430 us (0.75)
  matrix products: 246 us -> 17.8 us
  waiting for transfers between devices: 108 us -> 307 us
  local copies, waits for them, and re-layouts: 113 us -> 26.4 us
  Pallas kernels: 0 us -> 35.6 us
  other arithmetic: 33.1 us -> 9.07 us
  starting transfers between devices: 39.5 us -> 18.2 us
  loops' own time: 11.8 us -> 0 us
    dot_general x107 -> x3, matrix products: 246 us -> 17.8 us  [the longest x1 6.73 us: per_device(): lax.dot_general(piece, grad_out, NT, preferred_element_type=F32).astype(BF)]
    reduce_scatter x1, waiting for transfers between devices: 0.01 us -> 144 us  [per_device(): lax.psum_scatter(weight_part, 'sp', scatter_dimension=0, tiled=True)]
    ppermute x0 -> x8, waiting for transfers between devices: none -> 93.1 us  [the longest x4 93.1 us: per_device(): lax.ppermute(kv, 'sp', [(i, (i + s) % n) for i in range(n)])]
    reshape x48 -> x1, local copies, waits for them, and re-layouts: 72.3 us -> 0.92 us  [list_terms(): return jnp.repeat(term, SIZE, axis=2)]
    all_to_all x8 -> x1, waiting for transfers between devices: 69.8 us -> 0.01 us  [per_device(): lax.all_to_all(list_terms(key_blocks[0, 0], block_counts[0, 0]), 'sp', sp...]
    pallas_call x0 -> x2, Pallas kernels: none -> 35.6 us  [the longest x1 19.4 us: call_backward(): pl.pallas_call(backward_kernel, grid=(8,), in_specs=[pl.BlockSpec((TOK, 2...]
    all_to_all x8 -> x1, starting transfers between devices: 39 us -> 5.56 us  [per_device(): lax.all_to_all(list_terms(key_blocks[0, 0], block_counts[0, 0]), 'sp', sp...]
    reduce_sum x50 -> x2, other arithmetic: 24.7 us -> 0.18 us  [documents(): jnp.sum((positions[:, None] >= starts[None, :]).astype(jnp.int32), axis=1...]
  transfers between devices with their start and end apart: 11 -> 12, of which waited for: 8 -> 4; matrix products, arithmetic and copies ran while one was open for 66% -> 9% of each run, Pallas kernels for 0% -> 8%
where the time goes in v1:
time: 430 us; the launch traced here: 428 us
  waiting for transfers between devices  307 us (71%)
  Pallas kernels  35.6 us (8%)
  local copies, waits for them, and re-layouts  26.4 us (6%)
  starting transfers between devices  18.2 us (4%)
  matrix products  17.8 us (4%)
  between operations  14.2 us (3%)
  other arithmetic  9.07 us (2%)
    reduce_scatter x1, waiting for transfers between devices, per_device(): lax.psum_scatter(weight_part, 'sp', scatter_dimension=0, tiled=True)  144 us
    ppermute x4, waiting for transfers between devices, per_device(): lax.ppermute(kv, 'sp', [(i, (i + s) % n) for i in range(n)])  93.1 us
    psum x1, waiting for transfers between devices, per_device(): summed = lax.psum(shard_rows, 'dp').astype(F32)  56.8 us
    pallas_call x1, Pallas kernels, call_backward(): pl.pallas_call(backward_kernel, grid=(8,), in_specs=[pl.BlockSpec((TOK, 2...  19.4 us
    unnamed x49, local copies, waits for them, and re-layouts  17.5 us
    pallas_call x1, Pallas kernels, call_forward(): pl.pallas_call(forward_kernel, grid=(8,), in_specs=[pl.BlockSpec((TOK, 2...  16.3 us
    all_gather x1, waiting for transfers between devices, per_device(): piece = lax.all_gather(out_weight, 'sp', axis=0, tiled=True)  12.7 us
  transfers between devices with their start and end apart: 12, of which 4 were waited for; matrix products, arithmetic and copies ran while one was open for 9% of the time, Pallas kernels for 8%

profile of v1, /device:TPU:1, one launch (start us, length us, event | category | flops | bytes accessed | tf_op | source)
XLA Modules:
  0.0 428.4 jit_solution(11068155257350279845)
XLA Ops:
  7.3 0.7 all-gather.2.cloned.1.call-update
  7.9 2.3 pad_maximum_fusion
  10.2 2.5 collective-permute-start
  12.7 2.5 collective-permute-start.1
  15.2 1.9 collective-permute-start.2
  17.0 0.6 collective-permute-start.3
  17.7 0.1 copy.20
  17.8 0.2 copy.21
  18.0 0.3 broadcast_in_dim.35
  18.3 0.9 reshape.163
  19.2 5.6 %all-to-all-start = ((f32[16,16,256]{2,1,0:T(8,128)}), f32[16,16,256]{2,1,0:T(8,128)S(1)}, u32[]{:S(2)}, u32[]{:S(2)}) async-start(f32[16,16,256]{2,1,0:T(8,128)} %reshape.163), calls=%async_computation | async-start | bytes 524288 | tf_op jit(solution)/shard_map/all_to_all | solution.py:165
  24.9 0.2 reduce-window_clone.1
  25.1 0.1 convert_reduce_fusion.1
  25.2 0.1 convert_reduce_fusion
  25.3 0.6 pad_add_fusion
  25.9 0.9 copy.22.dk_ref
  26.9 93.1 %collective-permute-done = bf16[256,2048]{1,0:T(8,128)(2,1)S(1)} collective-permute-done((bf16[256,2048]{1,0:T(8,128)(2,1)}, bf16[256,2048]{1,0:T(8,128)(2,1)S(1)}, u32[]{:S(2)}, u32[]{:S(2)}) %collective-permute-start) | collective-permute-done | bytes 1048608 | tf_op jit(solution)/shard_map/ppermute | solution.py:167
  120.2 1.7 constant_dynamic-update-slice_fusion.3
  121.9 1.3 constant_dynamic-update-slice_fusion.2
  123.2 1.3 constant_dynamic-update-slice_fusion.1
  124.6 0.1 constant_dynamic-update-slice_fusion
  124.7 2.9 fusion.6
  127.5 1.9 copy-done.2
  129.4 1.7 copy-done.4
  131.1 1.2 copy-done.6
  132.3 16.3 %shard_map.119 = (bf16[2048,256]{1,0:T(8,128)(2,1)S(1)}, bf16[256,2048]{1,0:T(8,128)(2,1)S(1)}, bf16[16,1280,256]{2,1,0:T(8,128)(2,1)S(1)}, f32[16,8,256]{2,1,0:T(8,128)S(1)}) custom-call(bf16[256,2048]{1,0:T(8,128)(2,1)S(1)} %bitcast.27, bf16[1280,1024]{1,0:T(8,128)(2,1)S(1)} %copy-done.4, bf16[1280,1024]{1,0:T(8,128)(2,1)S(1)} %copy-done.2, ...), custom_call_target="tpu_custom_call" | custom-call | flops 6000000000 | bytes 20000000 | tf_op jit(solution)/shard_map/pallas_call | solution.py:87
  148.6 3.9 copy-done.8
  152.5 1.0 copy-done.9
  153.5 0.7 copy-done.11
  154.1 6.5 %convolution_convert_fusion = bf16[2048,3072]{1,0:T(8,128)(2,1)} fusion(bf16[2048,256]{1,0:T(8,128)(2,1)S(1)} %get-tuple-element.39.attn_t_ref, bf16[1,256,3072]{2,1,0:T(8,128)(2,1)S(1)} %copy-done), kind=kOutput, calls=%fused_computation | convolution fusion | flops 3227516928 | bytes 15204352 | tf_op jit(solution)/shard_map/dot_general | solution.py:177
  160.7 0.2 all-reduce.3.cloned.1.call-start
  160.9 12.7 %all-gather.2.cloned.1.call-done = bf16[2048,3072]{1,0:T(8,128)(2,1)} async-done(((bf16[128,3072]{1,0:T(8,128)(2,1)}), bf16[2048,3072]{1,0:T(8,128)(2,1)}) %all-gather.2.cloned.1.call-update) | async-done | bytes 12582928 | tf_op jit(solution)/shard_map/all_gather | solution.py:164
  173.6 6.7 %convolution_convert_fusion.2.g_t_ref = bf16[2048,256]{1,0:T(8,128)(2,1)S(1)} fusion(bf16[2048,3072]{1,0:T(8,128)(2,1)} %all-gather.2.cloned.1.call-done, bf16[1,256,3072]{2,1,0:T(8,128)(2,1)S(1)} %copy-done), kind=kOutput, calls=%fused_computation.3 | convolution fusion | flops 3221749760 | bytes 15204352 | tf_op jit(solution)/shard_map/dot_general | solution.py:176
  180.4 19.4 %shard_map.120 = (bf16[256,2048]{1,0:T(8,128)(2,1)}, bf16[1280,1024]{1,0:T(8,128)(2,1)S(1)}, bf16[1280,1024]{1,0:T(8,128)(2,1)S(1)}) custom-call(bf16[256,2048]{1,0:T(8,128)(2,1)S(1)} %bitcast.28, bf16[1280,1024]{1,0:T(8,128)(2,1)S(1)} %copy-done.5, bf16[1280,1024]{1,0:T(8,128)(2,1)S(1)} %copy-done.3, bf16[16,1280,256]{2,1,0:T(8,128)(2,1)} %copy-done.8, ...), custom_call_target="tpu_custom_call" | custom-call | flops 10000000000 | bytes 30000000 | tf_op jit(solution)/shard_map/pallas_call | solution.py:117
  199.8 0.3 constant_dynamic-update-slice_fusion.6
  200.1 0.3 constant_dynamic-update-slice_fusion.5
  200.5 2.2 fusion.5
  202.7 2.3 copy-done.13
  205.0 2.7 collective-permute-start.7
  207.7 1.1 collective-permute-start.6
  208.8 0.6 collective-permute-start.5
  209.4 0.5 collective-permute-start.4
  209.9 4.6 %fusion = bf16[1,256,3072]{2,1,0:T(8,128)(2,1)} fusion(bf16[256,2048]{1,0:T(8,128)(2,1)S(1)} %copy-done.10, bf16[2048,3072]{1,0:T(8,128)(2,1)S(1)} %bitcast.37), kind=kOutput, calls=%fused_computation.2 | convolution fusion | flops 3222011904 | bytes 15204352 | tf_op jit(solution)/shard_map/dot_general | solution.py:175
  214.5 143.9 %reduce-scatter.2.cloned.1.call-done = bf16[128,3072]{1,0:T(8,128)(2,1)} async-done(((bf16[2048,3072]{1,0:T(8,128)(2,1)}), bf16[128,3072]{1,0:T(8,128)(2,1)}) %reduce-scatter.2.cloned.1.call-update) | async-done | bytes 786448 | tf_op jit(solution)/shard_map/reduce_scatter | solution.py:178
  358.4 3.2 add_convert_fusion
  361.6 1.0 slice_bitcast_fusion
  362.7 56.8 %all-reduce.3.cloned.1.call-done = bf16[128,3072]{1,0:T(8,128)(2,1)} async-done(((bf16[128,3072]{1,0:T(8,128)(2,1)}), bf16[128,3072]{1,0:T(8,128)(2,1)}) %all-reduce.3.cloned.1.call-update) | async-done | bytes 786448 | tf_op jit(solution)/shard_map/psum | solution.py:179
  419.5 2.4 convert_multiply_fusion
  (66 shorter events, 0.4 us)
Async XLA Ops:
  7.2 147.0 %copy-start = (bf16[1,256,3072]{2,1,0:T(8,128)(2,1)S(1)}, bf16[1,256,3072]{2,1,0:T(8,128)(2,1)}, u32[]{:S(2)}) copy-start(bf16[1,256,3072]{2,1,0:T(8,128)(2,1)} %param.19) | copy-start | bytes 4718596
  7.2 10.5 %copy-start.17 = (s32[1,1,32]{2,1,0:T(1,128)S(1)}, s32[1,1,32]{2,1,0:T(1,128)}, u32[]{:S(2)}) copy-start(s32[1,1,32]{2,1,0:T(1,128)} %param.16) | copy-start | bytes 388
  7.2 10.5 %copy-start.16 = (s32[1,1,32,8]{2,3,1,0:T(8,128)S(1)}, s32[1,1,32,8]{2,3,1,0:T(8,128)}, u32[]{:S(2)}) copy-start(s32[1,1,32,8]{2,3,1,0:T(8,128)} %param.15) | copy-start | bytes 3076
  7.2 17.7 %copy-start.18 = (s32[1,16]{1,0:T(1,128)S(1)}, s32[1,16]{1,0:T(1,128)}, u32[]{:S(2)}) copy-start(s32[1,16]{1,0:T(1,128)} %param.17) | copy-start | bytes 196
  7.2 166.4 %all-gather.2.cloned.1.call-start = ((), (), s32[]{:S(2)}) async-start(), calls=%async_computation.2 | async-start | bytes 13369344 | tf_op jit(solution)/shard_map/all_gather | solution.py:164
  10.2 109.8 %collective-permute-start = (bf16[256,2048]{1,0:T(8,128)(2,1)}, bf16[256,2048]{1,0:T(8,128)(2,1)S(1)}, u32[]{:S(2)}, u32[]{:S(2)}) collective-permute-start(bf16[256,2048]{1,0:T(8,128)(2,1)} %pad_maximum_fusion), channel_id=1, source_target_pairs={{0,4},{1,5},{2,6},{3,7},{4,8},{5,9},{6,10},{7,11},{8,12},{9,13},{1... | collective-permute-start | bytes 3145736 | tf_op jit(solution)/shard_map/ppermute | solution.py:167
  12.7 107.5 %collective-permute-start.1 = (bf16[256,2048]{1,0:T(8,128)(2,1)}, bf16[256,2048]{1,0:T(8,128)(2,1)}, u32[]{:S(2)}, u32[]{:S(2)}) collective-permute-start(bf16[256,2048]{1,0:T(8,128)(2,1)} %pad_maximum_fusion), channel_id=1, source_target_pairs={{0,3},{1,4},{2,5},{3,6},{4,7},{5,8},{6,9},{7,10},{8,11},{9,12},{10... | collective-permute-start | bytes 3145736 | tf_op jit(solution)/shard_map/ppermute | solution.py:167
  15.2 106.7 %collective-permute-start.2 = (bf16[256,2048]{1,0:T(8,128)(2,1)}, bf16[256,2048]{1,0:T(8,128)(2,1)}, u32[]{:S(2)}, u32[]{:S(2)}) collective-permute-start(bf16[256,2048]{1,0:T(8,128)(2,1)} %pad_maximum_fusion), channel_id=1, source_target_pairs={{0,2},{1,3},{2,4},{3,5},{4,6},{5,7},{6,8},{7,9},{8,10},{9,11},{10,... | collective-permute-start | bytes 3145736 | tf_op jit(solution)/shard_map/ppermute | solution.py:167
  17.0 106.2 %collective-permute-start.3 = (bf16[256,2048]{1,0:T(8,128)(2,1)}, bf16[256,2048]{1,0:T(8,128)(2,1)}, u32[]{:S(2)}, u32[]{:S(2)}) collective-permute-start(bf16[256,2048]{1,0:T(8,128)(2,1)} %pad_maximum_fusion), channel_id=1, source_target_pairs={{0,1},{1,2},{2,3},{3,4},{4,5},{5,6},{6,7},{7,8},{8,9},{9,10},{10,1... | collective-permute-start | bytes 3145736 | tf_op jit(solution)/shard_map/ppermute | solution.py:167
  19.2 108.3 %all-to-all-start = ((f32[16,16,256]{2,1,0:T(8,128)}), f32[16,16,256]{2,1,0:T(8,128)S(1)}, u32[]{:S(2)}, u32[]{:S(2)}) async-start(f32[16,16,256]{2,1,0:T(8,128)} %reshape.163), calls=%async_computation | async-start | bytes 524288 | tf_op jit(solution)/shard_map/all_to_all | solution.py:165
  24.8 333.6 %reduce-scatter.2.cloned.1.call-start = ((), (), s32[]{:S(2)}) async-start(), calls=%async_computation.3 | async-start | bytes 13369344 | tf_op jit(solution)/shard_map/reduce_scatter | solution.py:178
  120.1 4.4 %copy-start.14 = (bf16[1,256,1024]{2,1,0:T(8,128)(2,1)S(1)}, bf16[1,256,1024]{2,1,0:T(8,128)(2,1)}, u32[]{:S(2)}) copy-start(bf16[1,256,1024]{2,1,0:T(8,128)(2,1)} %param.14) | copy-start | bytes 1572868
  120.1 4.4 %copy-start.15 = (bf16[1,256,1024]{2,1,0:T(8,128)(2,1)S(1)}, bf16[1,256,1024]{2,1,0:T(8,128)(2,1)}, u32[]{:S(2)}) copy-start(bf16[1,256,1024]{2,1,0:T(8,128)(2,1)} %param.13) | copy-start | bytes 1572868
  127.5 1.9 copy-start.2
  129.4 1.7 copy-start.4
  131.1 1.2 copy-start.6
  148.6 3.9 copy-start.8
  152.5 1.0 copy-start.9
  153.5 0.7 copy-start.11
  160.7 19.7 %copy-start.12 = (f32[16,8,256]{2,1,0:T(8,128)S(1)}, f32[16,8,256]{2,1,0:T(8,128)}, u32[]{:S(2)}) copy-start(f32[16,8,256]{2,1,0:T(8,128)} %copy-done.11) | copy-start | bytes 393220
  160.7 258.8 %all-reduce.3.cloned.1.call-start = ((), (), s32[]{:S(2)}) async-start(), calls=%async_computation.4 | async-start | bytes 1572864 | tf_op jit(solution)/shard_map/psum | solution.py:179
  173.6 6.8 %copy-start.3 = (bf16[1280,1024]{1,0:T(8,128)(2,1)S(1)}, bf16[1280,1024]{1,0:T(8,128)(2,1)}, u32[]{:S(2)}) copy-start(bf16[1280,1024]{1,0:T(8,128)(2,1)} %get-tuple-element.47.v_ref) | copy-start | bytes 7864324
  173.6 6.8 %copy-start.5 = (bf16[1280,1024]{1,0:T(8,128)(2,1)S(1)}, bf16[1280,1024]{1,0:T(8,128)(2,1)}, u32[]{:S(2)}) copy-start(bf16[1280,1024]{1,0:T(8,128)(2,1)} %get-tuple-element.48.k_ref) | copy-start | bytes 7864324
  173.6 6.8 %copy-start.7 = (bf16[1,256,2048]{2,1,0:T(8,128)(2,1)S(1)}, bf16[1,256,2048]{2,1,0:T(8,128)(2,1)}, u32[]{:S(2)}) copy-start(bf16[1,256,2048]{2,1,0:T(8,128)(2,1)} %param.12) | copy-start | bytes 3145732
  180.4 29.5 %slice-start = ((s8[12582912]{0:T(1024)(128)(4,1)}), s8[4194304]{0:T(1024)(128)(4,1)S(1)}, s32[]{:S(2)}) async-start(s8[12582912]{0:T(1024)(128)(4,1)} %bitcast.36), calls=%async_computation.5 | async-start | bytes 8388608
  180.4 29.5 %slice-start.1 = ((s8[12582912]{0:T(1024)(128)(4,1)}), s8[4194304]{0:T(1024)(128)(4,1)S(1)}, s32[]{:S(2)}) async-start(s8[12582912]{0:T(1024)(128)(4,1)} %bitcast.36), calls=%async_computation.6 | async-start | bytes 8388608
  199.8 10.1 %slice-start.2 = ((s8[12582912]{0:T(1024)(128)(4,1)}), s8[4194304]{0:T(1024)(128)(4,1)S(1)}, s32[]{:S(2)}) async-start(s8[12582912]{0:T(1024)(128)(4,1)} %bitcast.36), calls=%async_computation.7 | async-start | bytes 8388608
  200.5 4.5 %copy-start.13 = (bf16[1280,2048]{1,0:T(8,128)(2,1)}, bf16[1280,2048]{1,0:T(8,128)(2,1)S(1)}, u32[]{:S(2)}) copy-start(bf16[1280,2048]{1,0:T(8,128)(2,1)S(1)} %constant_dynamic-update-slice_fusion.5) | copy-start | bytes 15728644
  200.5 9.4 %copy-start.10 = (bf16[256,2048]{1,0:T(8,128)(2,1)S(1)}, bf16[256,2048]{1,0:T(8,128)(2,1)}, u32[]{:S(2)}) copy-start(bf16[256,2048]{1,0:T(8,128)(2,1)} %copy-done.9) | copy-start | bytes 3145732
  205.0 153.4 %collective-permute-start.7 = (bf16[256,2048]{1,0:T(8,128)(2,1)}, bf16[256,2048]{1,0:T(8,128)(2,1)S(1)}, u32[]{:S(2)}, u32[]{:S(2)}) collective-permute-start(bf16[256,2048]{1,0:T(8,128)(2,1)} %get-tuple-element.44), channel_id=1, source_target_pairs={{0,15},{1,0},{2,1},{3,2},{4,3},{5,4},{6,5},{7,6},{8,7},{9,8},{10,9... | collective-permute-start | bytes 3145736 | tf_op jit(solution)/shard_map/ppermute | solution.py:186
  207.7 150.7 %collective-permute-start.6 = (bf16[256,2048]{1,0:T(8,128)(2,1)}, bf16[256,2048]{1,0:T(8,128)(2,1)}, u32[]{:S(2)}, u32[]{:S(2)}) collective-permute-start(bf16[256,2048]{1,0:T(8,128)(2,1)} %get-tuple-element.45), channel_id=1, source_target_pairs={{0,14},{1,15},{2,0},{3,1},{4,2},{5,3},{6,4},{7,5},{8,6},{9,7},{10,... | collective-permute-start | bytes 3145736 | tf_op jit(solution)/shard_map/ppermute | solution.py:186
  208.8 149.6 %collective-permute-start.5 = (bf16[256,2048]{1,0:T(8,128)(2,1)}, bf16[256,2048]{1,0:T(8,128)(2,1)}, u32[]{:S(2)}, u32[]{:S(2)}) collective-permute-start(bf16[256,2048]{1,0:T(8,128)(2,1)} %get-tuple-element.46), channel_id=1, source_target_pairs={{0,13},{1,14},{2,15},{3,0},{4,1},{5,2},{6,3},{7,4},{8,5},{9,6},{10... | collective-permute-start | bytes 3145736 | tf_op jit(solution)/shard_map/ppermute | solution.py:186
  209.4 149.1 %collective-permute-start.4 = (bf16[256,2048]{1,0:T(8,128)(2,1)}, bf16[256,2048]{1,0:T(8,128)(2,1)}, u32[]{:S(2)}, u32[]{:S(2)}) collective-permute-start(bf16[256,2048]{1,0:T(8,128)(2,1)} %get-tuple-element.43), channel_id=1, source_target_pairs={{0,12},{1,13},{2,14},{3,15},{4,0},{5,1},{6,2},{7,3},{8,4},{9,5},{1... | collective-permute-start | bytes 3145736 | tf_op jit(solution)/shard_map/ppermute | solution.py:186
  358.4 63.5 %copy-start.1 = (bf16[1,256,3072]{2,1,0:T(8,128)(2,1)S(1)}, bf16[1,256,3072]{2,1,0:T(8,128)(2,1)}, u32[]{:S(2)}) copy-start(bf16[1,256,3072]{2,1,0:T(8,128)(2,1)} %param.19) | copy-start | bytes 4718596
Sparse Core Ops, SparseCore 0:
  10.2 163.3 all-gather.1
  177.0 181.2 reduce-scatter.1
  360.7 58.6 all-reduce.2

commit v2 on v1

--- a/solution.py
+++ b/solution.py
@@ -61,7 +61,7 @@
     forward_body(q_ref, k_ref, v_ref, list_ref, bias_ref, attn_t_ref, attn_ref, p_ref, r_ref)
 
 
-def backward_kernel(q_ref, k_ref, v_ref, p_ref, r_ref, attn_t_ref, g_t_ref, dq_ref, dk_ref, dv_ref):
+def backward_kernel(q_ref, k_ref, v_ref, p_ref, r_ref, attn_t_ref, g_t_ref, dq_ref, dkv_ref):
     scale = 1.0 / math.sqrt(SIZE)
     dk = jnp.zeros((BAND, SIZE), F32)
     dv = jnp.zeros((BAND, SIZE), F32)
@@ -79,8 +79,8 @@
         dq_ref[:, lanes] = (dq_t * scale).T.astype(BF)
         dk = dk + jnp.dot(ds, q_ref[:, lanes], preferred_element_type=F32)
         dv = dv + jnp.dot(p, g, preferred_element_type=F32)
-    dk_ref[...] = (dk * scale).astype(BF)
-    dv_ref[...] = dv.astype(BF)
+    dkv_ref[0] = (dk * scale).astype(BF)
+    dkv_ref[1] = dv.astype(BF)
 
 
 def call_forward(q, k, v, lists, dq, dk):
@@ -128,13 +128,11 @@
         ],
         out_specs=[
             pl.BlockSpec((TOK, 2 * SIZE), lambda c: (0, c)),
-            pl.BlockSpec((BAND, SIZE), lambda c: (0, c)),
-            pl.BlockSpec((BAND, SIZE), lambda c: (0, c)),
+            pl.BlockSpec((2, BAND, SIZE), lambda c: (0, 0, c)),
         ],
         out_shape=[
             jax.ShapeDtypeStruct((TOK, 2048), BF),
-            jax.ShapeDtypeStruct((BAND, 1024), BF),
-            jax.ShapeDtypeStruct((BAND, 1024), BF),
+            jax.ShapeDtypeStruct((2, BAND, 1024), BF),
         ],
         compiler_params=pltpu.CompilerParams(vmem_limit_bytes=32 * 2**20),
         cost_estimate=pl.CostEstimate(flops=10 * 10**9, bytes_accessed=30 * 10**6, transcendentals=0),
@@ -156,37 +154,353 @@
     return jnp.repeat(term, SIZE, axis=2)
 
 
+MESH = pl.DeviceIdType.MESH
+HALF = 1536
+PART = 384
+
+
+def place():
+    dp = lax.axis_index("dp")
+    sp = lax.axis_index("sp")
+    return dp, sp, sp // 4, sp % 4
+
+
+def sp_at(z, x):
+    return (z + 4) % 4 * 4 + (x + 4) % 4
+
+
+def dp_at(y, core):
+    return (y + 4) % 4 * 2 + core
+
+
+def greet():
+    dp, sp, _, _ = place()
+    barrier = pltpu.get_barrier_semaphore()
+    for r in range(1, 16):
+        pl.semaphore_signal(barrier, inc=1, device_id=(dp, (sp + r) % 16), device_id_type=MESH)
+    for r in range(1, 8):
+        pl.semaphore_signal(barrier, inc=1, device_id=((dp + r) % 8, sp), device_id_type=MESH)
+    pl.semaphore_wait(barrier, 22)
+
+
+def remote(src, dst, send, recv, dp, sp):
+    return pltpu.make_async_remote_copy(
+        src_ref=src, dst_ref=dst, send_sem=send, recv_sem=recv, device_id=(dp, sp), device_id_type=MESH
+    )
+
+
+class Sends:
+    def __init__(self, sems):
+        self.sems = sems
+        self.started = []
+
+    def go(self, src, dst, recv, dp, sp, when=None):
+        copy = remote(src, dst, self.sems.at[len(self.started)], recv, dp, sp)
+        self.started.append((copy, when))
+        if when is None:
+            copy.start()
+        else:
+            pl.when(when)(copy.start)
+
+    def finish(self):
+        for copy, when in self.started:
+            if when is None:
+                copy.wait_send()
+            else:
+                pl.when(when)(copy.wait_send)
+
+
+def arrived(dst, recv):
+    dp, sp, _, _ = place()
+    remote(dst, dst, recv, recv, dp, sp).wait_recv()
+
+
+def gather_kernel(
+    k_ref, v_ref, lists_ref, w_ref, d_ref, kb_ref, vb_ref, lb_ref, wb_ref, db_ref, send, kv_recv, w_recv, pair_recv, l_recv, d_recv, local
+):
+    dp, sp, z, x = place()
+    core = dp % 2
+    other = dp + 1 - 2 * core
+    cols = pl.ds(pl.multiple_of(core * HALF, HALF), HALF)
+    part = lambda e: pl.ds(pl.multiple_of(e * PART, PART), PART)
+    locals_ = [
+        pltpu.make_async_copy(k_ref, kb_ref.at[4], local.at[0]),
+        pltpu.make_async_copy(v_ref, vb_ref.at[4], local.at[1]),
+        pltpu.make_async_copy(lists_ref.at[sp], lb_ref.at[sp], local.at[2]),
+        pltpu.make_async_copy(w_ref, wb_ref.at[sp], local.at[3]),
+        pltpu.make_async_copy(d_ref.at[:, part(dp)], db_ref.at[dp], local.at[4]),
+    ]
+    greet()
+    out = Sends(send)
+
+    def kv(which, src, slot, to, when=None):
+        band = (kb_ref, vb_ref)[which]
+        out.go(src, band.at[slot], kv_recv.at[which, slot], dp, to, when)
+
+    own = (k_ref, v_ref)
+    bands = (kb_ref, vb_ref)
+    right, left = sp_at(z, x + 1), sp_at(z, x - 1)
+    up, down = sp_at(z + 1, x), sp_at(z - 1, x)
+    top, bottom = pl.ds(0, 64), pl.ds(64, 64)
+
+    def weight(slot, rows, to):
+        block = wb_ref.at[slot, rows, cols]
+        out.go(block, block, w_recv.at[slot], dp, to)
+
+    def weight_own(to):
+        out.go(w_ref.at[:, cols], wb_ref.at[sp, :, cols], w_recv.at[sp], dp, to)
+
+    def pair(slot):
+        block = wb_ref.at[slot, :, cols]
+        out.go(block, block, pair_recv.at[slot], other, sp)
+
+    def weight_here(slot):
+        arrived(wb_ref.at[slot, :, cols], w_recv.at[slot])
+
+    weight_own(right)
+    weight_own(left)
+    for i in (0, 1):
+        kv(i, own[i], 0, up)
+    for i in (0, 1):
+        kv(i, own[i], 3, right, x < 3)
+        kv(i, own[i], 1, left, x == 0)
+    weight_own(up)
+    weight_own(down)
+    for r in range(1, 16):
+        to = (sp + r) % 16
+        out.go(lists_ref.at[to], lb_ref.at[sp], l_recv, dp, to)
+    for copy in locals_:
+        copy.start()
+    for r in range(1, 8):
+        to = (dp + r) % 8
+        out.go(d_ref.at[:, part(to)], db_ref.at[dp], d_recv, to, sp)
+
+    whole = pl.ds(0, 128)
+    a, b, c = sp_at(z, x - 1), sp_at(z, x + 1), sp_at(z, x + 2)
+    weight_here(a)
+    weight(a, top, right)
+    weight(a, whole, up)
+    weight(a, whole, down)
+    weight_here(b)
+    weight(b, bottom, left)
+    weight(b, whole, up)
+    weight(b, whole, down)
+    pair(a)
+    pair(b)
+    for i in (0, 1):
+        arrived(bands[i].at[0], kv_recv.at[i, 0])
+        kv(i, bands[i].at[0], 3, right, x == 3)
+        kv(i, bands[i].at[0], 1, left, x > 0)
+    weight_here(c)
+    weight(c, whole, up)
+    weight(c, whole, down)
+    pair(c)
+    for i in (0, 1):
+        arrived(bands[i].at[3], kv_recv.at[i, 3])
+        kv(i, bands[i].at[3], 2, right, (x < 3) if i == 0 else (x == 2))
+        arrived(bands[i].at[1], kv_recv.at[i, 1])
+        kv(i, bands[i].at[1], 2, left, (x == 1) if i == 0 else (x > 0))
+    for dx in (0, -1, 1, 2):
+        below, above = sp_at(z - 1, x + dx), sp_at(z + 1, x + dx)
+        weight_here(below)
+        weight(below, top, up)
+        pair(below)
+        weight_here(above)
+        weight(above, bottom, down)
+        pair(above)
+    for i in (0, 1):
+        arrived(bands[i].at[2], kv_recv.at[i, 2])
+    for dx in (0, -1, 1, 2):
+        far = sp_at(z + 2, x + dx)
+        weight_here(far)
+        pair(far)
+    for r in range(1, 16):
+        slot = (sp + r) % 16
+        arrived(wb_ref.at[slot, :, pl.ds(pl.multiple_of((1 - core) * HALF, HALF), HALF)], pair_recv.at[slot])
+    arrived(lb_ref.at[pl.ds(0, 15)], l_recv)
+    arrived(db_ref.at[pl.ds(0, 7)], d_recv)
+    for copy in locals_:
+        copy.wait()
+    out.finish()
+
+
+ANY = pl.BlockSpec(memory_space=pl.ANY)
+DMA = pltpu.SemaphoreType.DMA
+
+
+def call_gather(k, v, lists, w, d):
+    return pl.pallas_call(
+        gather_kernel,
+        in_specs=[ANY] * 5,
+        out_specs=[ANY] * 5,
+        out_shape=[
+            jax.ShapeDtypeStruct((5, TOK, 1024), BF),
+            jax.ShapeDtypeStruct((5, TOK, 1024), BF),
+            jax.ShapeDtypeStruct((16, 16, TOK), F32),
+            jax.ShapeDtypeStruct((16, 128, 3072), BF),
+            jax.ShapeDtypeStruct((8, TOK, PART), BF),
+        ],
+        scratch_shapes=[DMA((80,)), DMA((2, 5)), DMA((16,)), DMA((16,)), DMA, DMA, DMA((5,))],
+        compiler_params=pltpu.CompilerParams(collective_id=0, has_side_effects=True),
+    )(k, v, lists, w, d)
+
+
+def spread_kernel(a_ref, ab_ref, send, recv, local):
+    dp, sp, _, _ = place()
+    y, core = dp // 2, dp % 2
+    other = dp_at(y, 1 - core)
+    copy = pltpu.make_async_copy(a_ref, ab_ref.at[dp], local)
+    greet()
+    out = Sends(send)
+    copy.start()
+    up, down = dp_at(y + 1, core), dp_at(y - 1, core)
+    far = dp_at(y + 2, core)
+    out.go(a_ref, ab_ref.at[dp], recv.at[dp], up, sp)
+    out.go(a_ref, ab_ref.at[dp], recv.at[dp], down, sp)
+    out.go(a_ref, ab_ref.at[dp], recv.at[dp], other, sp)
+
+    def on(slot, rows, to):
+        block = ab_ref.at[slot, rows]
+        out.go(block, block, recv.at[slot], to, sp)
+
+    for slot, rows, to in ((down, pl.ds(0, 1024), up), (up, pl.ds(1024, 1024), down)):
+        arrived(ab_ref.at[slot], recv.at[slot])
+        on(slot, rows, to)
+        on(slot, pl.ds(0, 2048), other)
+    arrived(ab_ref.at[far], recv.at[far])
+    on(far, pl.ds(0, 2048), other)
+    for r in range(4):
+        slot = dp_at(y + r, 1 - core)
+        arrived(ab_ref.at[slot], recv.at[slot])
+    copy.wait()
+    out.finish()
+
+
+def call_spread(attn_t):
+    return pl.pallas_call(
+        spread_kernel,
+        in_specs=[ANY],
+        out_specs=ANY,
+        out_shape=jax.ShapeDtypeStruct((8, 2048, TOK), BF),
+        scratch_shapes=[DMA((8,)), DMA((8,)), DMA],
+        compiler_params=pltpu.CompilerParams(collective_id=1, has_side_effects=True),
+    )(attn_t)
+
+
+def return_kernel(g_ref, b_ref, gb_ref, o_ref, rs, back, low, mine, gsum, send, rs_recv, g_recv, row_recv, z_recv, local):
+    dp, sp, z, x = place()
+    loads = [
+        pltpu.make_async_copy(g_ref.at[sp], rs.at[sp], local.at[0]),
+        pltpu.make_async_copy(b_ref.at[:, 0], low, local.at[1]),
+        pltpu.make_async_copy(b_ref.at[:, 4], mine, local.at[2]),
+    ]
+    greet()
+    out = Sends(send)
+    for copy in loads:
+        copy.start()
+    for k in (2, 1, 3):
+        out.go(b_ref.at[:, 4 - k], back.at[k - 1], row_recv.at[k - 1], dp, sp_at(z, x - k))
+    for r in range(1, 16):
+        to = (sp + r) % 16
+        out.go(g_ref.at[to], rs.at[sp], rs_recv, dp, to)
+    for copy in loads:
+        copy.wait()
+    arrived(rs.at[pl.ds(0, 15)], rs_recv)
+    total = rs[0].astype(F32)
+    for i in range(1, 16):
+        total = total + rs[i].astype(F32)
+    gsum[...] = total.astype(BF)
+    for r in range(1, 8):
+        out.go(gsum, gb_ref.at[dp], g_recv, (dp + r) % 8, sp)
+    final = pltpu.make_async_copy(gsum, gb_ref.at[dp], local.at[3])
+    final.start()
+    for k in (1, 2, 3):
+        arrived(back.at[k - 1], row_recv.at[k - 1])
+    keep = [jnp.where(x + k < 4, 1.0, 0.0).astype(F32) for k in (1, 2, 3)]
+
+    def rows_of(i):
+        return pl.ds(pl.multiple_of(i * 32, 32), 32)
+
+    def add(i, _):
+        w, rows = i // 8, rows_of(i % 8)
+        below = low[w, rows].astype(F32)
+        here = mine[w, rows].astype(F32)
+        for k in range(3):
+            got = back[k, w, rows].astype(F32)
+            here = here + got * keep[k]
+            below = below + got * (1.0 - keep[k])
+        low[w, rows] = below.astype(BF)
+        mine[w, rows] = here.astype(BF)
+        return 0
+
+    lax.fori_loop(0, 16, add, 0)
+    out.go(low, back.at[3], z_recv, dp, sp_at(z - 1, x))
+    arrived(gb_ref.at[pl.ds(0, 7)], g_recv)
+    final.wait()
+    arrived(back.at[3], z_recv)
+
+    def last(i, _):
+        w, rows = i // 8, rows_of(i % 8)
+        o_ref[w, rows] = (mine[w, rows].astype(F32) + back[3, w, rows].astype(F32)).astype(BF)
+        return 0
+
+    lax.fori_loop(0, 16, last, 0)
+    out.finish()
+
+
+def call_return(g, bands):
+    vmem = pl.BlockSpec(memory_space=pltpu.VMEM)
+    return pl.pallas_call(
+        return_kernel,
+        in_specs=[ANY, ANY],
+        out_specs=[ANY, vmem],
+        out_shape=[
+            jax.ShapeDtypeStruct((8, 128, PART), BF),
+            jax.ShapeDtypeStruct((2, TOK, 1024), BF),
+        ],
+        scratch_shapes=[
+            pltpu.VMEM((16, 128, PART), BF),
+            pltpu.VMEM((4, 2, TOK, 1024), BF),
+            pltpu.VMEM((2, TOK, 1024), BF),
+            pltpu.VMEM((2, TOK, 1024), BF),
+            pltpu.VMEM((128, PART), BF),
+            DMA((32,)),
+            DMA,
+            DMA,
+            DMA((3,)),
+            DMA,
+            DMA((4,)),
+        ],
+        compiler_params=pltpu.CompilerParams(collective_id=2, has_side_effects=True, vmem_limit_bytes=32 * 2**20),
+    )(g, bands)
+
+
 def per_device(queries, keys, values, key_blocks, block_counts, doc_lengths, out_weight, d_out):
     q = queries[0]
     grad_out = d_out[0]
     me = lax.axis_index("sp")
     n = lax.axis_size("sp")
-    piece = lax.all_gather(out_weight, "sp", axis=0, tiled=True)
-    lists = lax.all_to_all(list_terms(key_blocks[0, 0], block_counts[0, 0]), "sp", split_axis=0, concat_axis=0, tiled=True)
-    kv = jnp.concatenate([keys[0], values[0]], axis=1)
-    parts = [lax.ppermute(kv, "sp", [(i, (i + s) % n) for i in range(n)]) for s in range(HALO, 0, -1)]
-    band = jnp.concatenate(parts + [kv], axis=0)
-    k, v = band[:, :1024], band[:, 1024:]
+    lists = list_terms(key_blocks[0, 0], block_counts[0, 0])
+    k, v, lists, weight, grad_parts = call_gather(keys[0], values[0], lists, out_weight, grad_out)
+    k = k.reshape(BAND, 1024)
+    v = v.reshape(BAND, 1024)
+    weight = weight.reshape(2048, 3072)
     q_pos = me * TOK + jnp.arange(TOK, dtype=jnp.int32)
     k_pos = (me - HALO) * TOK + jnp.arange(BAND, dtype=jnp.int32)
     dq = jnp.zeros((8, TOK), jnp.int32).at[0].set(documents(q_pos, doc_lengths[0])).at[1].set(q_pos)
     dk = jnp.stack([documents(k_pos, doc_lengths[0]), k_pos], axis=1)
     attn_t, attn, p, r = call_forward(q, k, v, lists, dq, dk)
-    layer_out = jnp.dot(attn, piece, preferred_element_type=F32).astype(BF)
-    g_t = lax.dot_general(piece, grad_out, NT, preferred_element_type=F32).astype(BF)
-    weight_part = jnp.dot(attn_t, grad_out, preferred_element_type=F32).astype(BF)
-    shard_rows = lax.psum_scatter(weight_part, "sp", scatter_dimension=0, tiled=True)
-    summed = lax.psum(shard_rows, "dp").astype(F32)
-    grad_weight = summed * (1.0 / math.sqrt(lax.axis_size("dp") * n * TOK))
-    grad_q, dk_band, dv_band = call_backward(q, k, v, p, r, attn_t, g_t)
-    dkv = jnp.concatenate([dk_band, dv_band], axis=1)
-    total = dkv[HALO * TOK :].astype(F32)
-    for s in range(HALO, 0, -1):
-        piece_back = dkv[(HALO - s) * TOK : (HALO - s + 1) * TOK]
-        back = lax.ppermute(piece_back, "sp", [(i, (i - s) % n) for i in range(n)])
-        total = total + back.astype(F32)
-    total = total.astype(BF)
-    return (layer_out[None], grad_q[None], total[None, :, :1024], total[None, :, 1024:], grad_weight)
+    attn_all = call_spread(attn_t)
+    g_t = lax.dot_general(weight, grad_out, NT, preferred_element_type=F32).astype(BF)
+    grad_q, bands = call_backward(q, k, v, p, r, attn_t, g_t)
+    weight_part = lax.dot_general(
+        attn_all, grad_parts, (((0, 2), (0, 1)), ((), ())), preferred_element_type=F32
+    ).astype(BF)
+    grad_all, grad_kv = call_return(weight_part.reshape(16, 128, PART), bands.reshape(2, 5, TOK, 1024))
+    layer_out = jnp.dot(attn, weight, preferred_element_type=F32).astype(BF)
+    grad_weight = grad_all.transpose(1, 0, 2).reshape(128, 3072).astype(F32)
+    grad_weight = grad_weight * (1.0 / math.sqrt(lax.axis_size("dp") * n * TOK))
+    return (layer_out[None], grad_q[None], grad_kv[:1], grad_kv[1:], grad_weight)
 
 
 def solution(mesh):

time: 430 us -> 309 us (0.72)
  waiting for transfers between devices: 307 us -> 0 us
  Pallas kernels: 35.6 us -> 265 us
  starting transfers between devices: 18.2 us -> 0 us
  local copies, waits for them, and re-layouts: 26.4 us -> 11.8 us
  between operations: 14.2 us -> 0.91 us
  matrix products: 17.8 us -> 27.9 us
  other arithmetic: 9.07 us -> 1.98 us
    pallas_call x0 -> x3, Pallas kernels: none -> 230 us  [the longest x1 96.2 us: call_return(): pl.pallas_call(return_kernel, in_specs=[ANY, ANY], out_specs=[ANY, vmem],...]
    reduce_scatter x1 -> x0, waiting for transfers between devices: 144 us -> none  [per_device(): lax.psum_scatter(weight_part, 'sp', scatter_dimension=0, tiled=True)]
    ppermute x8 -> x0, waiting for transfers between devices: 93.1 us -> none  [the longest x4 93.1 us: per_device(): lax.ppermute(kv, 'sp', [(i, (i + s) % n) for i in range(n)])]
    psum x1 -> x0, waiting for transfers between devices: 56.8 us -> none  [per_device(): summed = lax.psum(shard_rows, 'dp').astype(F32)]
    all_gather x1 -> x0, waiting for transfers between devices: 12.7 us -> none  [per_device(): piece = lax.all_gather(out_weight, 'sp', axis=0, tiled=True)]
    ppermute x8 -> x0, starting transfers between devices: 12.3 us -> none  [the longest x4 7.43 us: per_device(): lax.ppermute(kv, 'sp', [(i, (i + s) % n) for i in range(n)])]
    dot_general x3, matrix products: 17.8 us -> 27.9 us  [the longest x1 13.2 us: per_device(): layer_out = jnp.dot(attn, weight, preferred_element_type=F32).astype(BF)]
    unnamed x49 -> x25, local copies, waits for them, and re-layouts: 17.5 us -> 8.46 us
  transfers between devices with their start and end apart: 12 -> 0, of which waited for: 4 -> 0; matrix products, arithmetic and copies ran while one was open for 9% -> 0% of each run, Pallas kernels for 8% -> 0%
where the time goes in v2:
time: 309 us; the launch traced here: 308 us
  Pallas kernels  265 us (86%)
  matrix products  27.9 us (9%)
  local copies, waits for them, and re-layouts  11.8 us (4%)
    pallas_call x1, Pallas kernels, call_return(): pl.pallas_call(return_kernel, in_specs=[ANY, ANY], out_specs=[ANY, vmem],...  96.2 us
    pallas_call x1, Pallas kernels, call_gather(): pl.pallas_call(gather_kernel, in_specs=[ANY] * 5, out_specs=[ANY] * 5, ou...  88.8 us
    pallas_call x1, Pallas kernels, call_spread(): pl.pallas_call(spread_kernel, in_specs=[ANY], out_specs=ANY, out_shape=ja...  44.6 us
    pallas_call x1, Pallas kernels, call_backward(): pl.pallas_call(backward_kernel, grid=(8,), in_specs=[pl.BlockSpec((TOK, 2...  19.2 us
    pallas_call x1, Pallas kernels, call_forward(): pl.pallas_call(forward_kernel, grid=(8,), in_specs=[pl.BlockSpec((TOK, 2...  16.3 us
    dot_general x1, matrix products, per_device(): layer_out = jnp.dot(attn, weight, preferred_element_type=F32).astype(BF)  13.2 us
    unnamed x25, local copies, waits for them, and re-layouts  8.46 us
    dot_general x1, matrix products, per_device(): lax.dot_general(attn_all, grad_parts, (((0, 2), (0, 1)), ((), ())), prefe...  8.05 us

profile of v2, /device:TPU:1, one launch (start us, length us, event | category | flops | bytes accessed | tf_op | source)
XLA Modules:
  0.0 307.6 jit_solution(226106317116211082)
XLA Ops:
  0.7 0.7 iota_compare_fusion
  1.3 0.7 and_reduce_fusion
  2.1 0.1 copy.24
  2.1 0.2 copy.25
  2.3 0.3 broadcast_in_dim.16
  2.6 0.0 copy-start.9
  2.7 0.9 reshape.182.lists_ref
  3.6 0.0 copy-start.4
  3.6 88.8 %shard_map.119 = (bf16[5,256,1024]{2,1,0:T(8,128)(2,1)}, bf16[5,256,1024]{2,1,0:T(8,128)(2,1)}, f32[16,16,256]{2,1,0:T(8,128)}, bf16[16,128,3072]{2,1,0:T(8,128)(2,1)}, bf16[8,256,384]{2,1,0:T(8,128)(2,1)}) custom-call(bf16[256,1024]{1,0:T(8,128)(2,1)} %bitcast.44, bf16[256,1024]{1,0:T(8,128)(2,1)} %bitcast.45, f32[16,16,256]{2,1,0:T(8,128)} %reshape.182.lists_ref, ...), custom_call_target="tpu_custom_call" | custom-call | tf_op jit(solution)/shard_map/pallas_call | solution.py:332
  92.4 0.0 copy-done.9
  92.4 0.2 reduce-window_clone.1
  92.6 0.1 convert_reduce_fusion.1
  92.8 0.1 convert_reduce_fusion
  92.9 0.3 copy.26.dk_ref
  93.2 0.0 copy-done.4
  93.2 0.0 copy-start.2
  93.2 1.7 copy-done.2
  95.0 0.0 copy-start.3
  95.0 1.7 copy-done.3
  96.7 0.0 copy-start.5
  96.7 0.9 copy-done.5
  97.6 16.3 %shard_map.120 = (bf16[2048,256]{1,0:T(8,128)(2,1)S(1)}, bf16[256,2048]{1,0:T(8,128)(2,1)S(1)}, bf16[16,1280,256]{2,1,0:T(8,128)(2,1)S(1)}, f32[16,8,256]{2,1,0:T(8,128)S(1)}) custom-call(bf16[256,2048]{1,0:T(8,128)(2,1)S(1)} %bitcast.40, bf16[1280,1024]{1,0:T(8,128)(2,1)S(1)} %bitcast.36, bf16[1280,1024]{1,0:T(8,128)(2,1)S(1)} %bitcast.38, ...), custom_call_target="tpu_custom_call" | custom-call | flops 6000000000 | bytes 20000000 | tf_op jit(solution)/shard_map/pallas_call | solution.py:87
  113.9 0.0 copy-start.6
  113.9 0.0 copy-start.1
  113.9 0.0 copy-start.7
  114.0 13.2 %fusion = bf16[1,256,3072]{2,1,0:T(8,128)(2,1)} fusion(bf16[256,2048]{1,0:T(8,128)(2,1)S(1)} %get-tuple-element.45, bf16[2048,3072]{1,0:T(8,128)(2,1)} %bitcast.49), kind=kOutput, calls=%fused_computation.1 | convolution fusion | flops 3222011904 | bytes 15204352 | tf_op jit(solution)/shard_map/dot_general | solution.py:500
  127.2 0.0 copy-done.6
  127.2 0.0 copy-done.7
  127.2 6.6 %convolution_convert_fusion.1.g_t_ref = bf16[2048,256]{1,0:T(8,128)(2,1)S(1)} fusion(bf16[2048,3072]{1,0:T(8,128)(2,1)} %bitcast.50, bf16[1,256,3072]{2,1,0:T(8,128)(2,1)S(1)} %copy-done.7), kind=kOutput, calls=%fused_computation.3 | convolution fusion | flops 3221749760 | bytes 15204352 | tf_op jit(solution)/shard_map/dot_general | solution.py:494
  133.8 0.0 copy-done.1
  133.8 19.2 %shard_map.121 = (bf16[256,2048]{1,0:T(8,128)(2,1)}, bf16[2,1280,1024]{2,1,0:T(8,128)(2,1)S(1)}) custom-call(bf16[256,2048]{1,0:T(8,128)(2,1)S(1)} %bitcast.41, bf16[1280,1024]{1,0:T(8,128)(2,1)S(1)} %bitcast.37, bf16[1280,1024]{1,0:T(8,128)(2,1)S(1)} %bitcast.39, bf16[16,1280,256]{2,1,0:T(8,128)(2,1)} %copy-done.6, ...), custom_call_target="tpu_custom_call" | custom-call | flops 10000000000 | bytes 30000000 | tf_op jit(solution)/shard_map/pallas_call | solution.py:117
  153.0 0.0 copy-start
  153.0 2.4 copy-done
  155.4 0.0 copy-start.8
  155.4 44.6 %shard_map.122 = bf16[8,2048,256]{2,1,0:T(8,128)(2,1)} custom-call(bf16[2048,256]{1,0:T(8,128)(2,1)} %copy-done.1), custom_call_target="tpu_custom_call" | custom-call | tf_op jit(solution)/shard_map/pallas_call | solution.py:380
  199.9 0.0 slice-start
  199.9 0.0 copy-done.8
  200.0 0.0 slice-start.1
  200.0 8.1 %bitcast_convert_fusion = bf16[2048,384]{1,0:T(8,128)(2,1)S(1)} fusion(bf16[8,2048,256]{2,1,0:T(8,128)(2,1)} %shard_map.122, bf16[8,256,384]{2,1,0:T(8,128)(2,1)S(1)} %copy-done.8), kind=kOutput, calls=%fused_computation.2 | convolution fusion | flops 3222011904 | bytes 11534336 | tf_op jit(solution)/shard_map/dot_general | solution.py:496
  208.0 0.0 slice-done
  208.0 0.0 slice-done.1
  208.1 96.2 %shard_map.123 = (bf16[8,128,384]{2,1,0:T(8,128)(2,1)S(1)}, bf16[2,256,1024]{2,1,0:T(8,128)(2,1)S(1)}) custom-call(bf16[16,128,384]{2,1,0:T(8,128)(2,1)S(1)} %bitcast.35, bf16[2,5,256,1024]{3,2,1,0:T(8,128)(2,1)S(1)} %bitcast.34), custom_call_target="tpu_custom_call" | custom-call | tf_op jit(solution)/shard_map/pallas_call | solution.py:453
  304.3 1.0 fusion.4
  305.3 0.2 multiply_bitcast_fusion
  305.5 0.5 copy.27
  305.9 1.6 copy.28
  (15 shorter events, 0.1 us)
Async XLA Ops:
  2.6 89.8 %copy-start.9 = (s32[1,16]{1,0:T(1,128)S(1)}, s32[1,16]{1,0:T(1,128)}, u32[]{:S(2)}) copy-start(s32[1,16]{1,0:T(1,128)} %param.17) | copy-start | bytes 196
  3.6 89.6 %copy-start.4 = (bf16[1,256,2048]{2,1,0:T(8,128)(2,1)S(1)}, bf16[1,256,2048]{2,1,0:T(8,128)(2,1)}, u32[]{:S(2)}) copy-start(bf16[1,256,2048]{2,1,0:T(8,128)(2,1)} %param.12) | copy-start | bytes 3145732
  93.2 1.7 copy-start.2
  95.0 1.7 copy-start.3
  96.7 0.9 copy-start.5
  113.9 13.3 %copy-start.6 = (bf16[16,1280,256]{2,1,0:T(8,128)(2,1)}, bf16[16,1280,256]{2,1,0:T(8,128)(2,1)S(1)}, u32[]{:S(2)}) copy-start(bf16[16,1280,256]{2,1,0:T(8,128)(2,1)S(1)} %get-tuple-element.47.p_ref) | copy-start | bytes 31457284
  113.9 19.9 %copy-start.1 = (bf16[2048,256]{1,0:T(8,128)(2,1)}, bf16[2048,256]{1,0:T(8,128)(2,1)S(1)}, u32[]{:S(2)}) copy-start(bf16[2048,256]{1,0:T(8,128)(2,1)S(1)} %get-tuple-element.49.attn_t_ref.a_ref) | copy-start | bytes 3145732
  113.9 13.3 %copy-start.7 = (bf16[1,256,3072]{2,1,0:T(8,128)(2,1)S(1)}, bf16[1,256,3072]{2,1,0:T(8,128)(2,1)}, u32[]{:S(2)}) copy-start(bf16[1,256,3072]{2,1,0:T(8,128)(2,1)} %param.19) | copy-start | bytes 4718596
  153.0 2.4 copy-start
  155.4 44.6 %copy-start.8 = (bf16[8,256,384]{2,1,0:T(8,128)(2,1)S(1)}, bf16[8,256,384]{2,1,0:T(8,128)(2,1)}, u32[]{:S(2)}) copy-start(bf16[8,256,384]{2,1,0:T(8,128)(2,1)} %get-tuple-element.51) | copy-start | bytes 4718596
  199.9 8.1 %slice-start = ((s8[5242880]{0:T(1024)(128)(4,1)}), s8[4194304]{0:T(1024)(128)(4,1)S(1)}, s32[]{:S(2)}) async-start(s8[5242880]{0:T(1024)(128)(4,1)} %bitcast.32), calls=%async_computation | async-start | bytes 8388608
  200.0 8.1 %slice-start.1 = ((s8[5242880]{0:T(1024)(128)(4,1)}), s8[1048576]{0:T(1024)(128)(4,1)S(1)}, s32[]{:S(2)}) async-start(s8[5242880]{0:T(1024)(128)(4,1)} %bitcast.32), calls=%async_computation.1 | async-start | bytes 2097152

commit v3 on v1

v3 whole, which is shorter than its diff:
```python
import math

import jax
import jax.numpy as jnp
from jax import lax
from jax.experimental import pallas as pl
from jax.experimental.pallas import tpu as pltpu
from jax.sharding import PartitionSpec as P

SIZE = 128
TOK = 256
HALO = 4
BAND = (HALO + 1) * TOK
KB = BAND // SIZE
NEG = -1e30
BF = jnp.bfloat16
F32 = jnp.float32
NT = (((1,), (1,)), ((), ()))
TN = (((0,), (0,)), ((), ()))


def list_terms(key_blocks, block_counts):
    slots = jnp.arange(8, dtype=jnp.int32)
    used = slots[None, :] < block_counts[:, None]
    device = jnp.arange(32, dtype=jnp.int32) // 2
    band = 2 * device[:, None] - 2 * HALO + jnp.arange(16, dtype=jnp.int32)[None, :]
    listed = jnp.any((key_blocks[:, None, :] == band[:, :, None]) & used[:, None, :], axis=2)
    term = jnp.where(listed, 0.0, NEG).astype(F32).reshape(16, 2, 16).transpose(0, 2, 1)
    return jnp.repeat(term, SIZE, axis=2)


MESH = pl.DeviceIdType.MESH
HALF = 1536
PART = 384


def place():
    dp = lax.axis_index("dp")
    sp = lax.axis_index("sp")
    return dp, sp, sp // 4, sp % 4


def sp_at(z, x):
    return (z + 4) % 4 * 4 + (x + 4) % 4


def dp_at(y, core):
    return (y + 4) % 4 * 2 + core


def greet():
    dp, sp, _, _ = place()
    barrier = pltpu.get_barrier_semaphore()
    for r in range(1, 16):
        pl.semaphore_signal(barrier, inc=1, device_id=(dp, (sp + r) % 16), device_id_type=MESH)
    for r in range(1, 8):
        pl.semaphore_signal(barrier, inc=1, device_id=((dp + r) % 8, sp), device_id_type=MESH)
    pl.semaphore_wait(barrier, 22)


def remote(src, dst, send, recv, dp, sp):
    return pltpu.make_async_remote_copy(
        src_ref=src, dst_ref=dst, send_sem=send, recv_sem=recv, device_id=(dp, sp), device_id_type=MESH
    )


class Sends:
    def __init__(self, sems):
        self.sems = sems
        self.started = []

    def go(self, src, dst, recv, dp, sp, when=None):
        copy = remote(src, dst, self.sems.at[len(self.started)], recv, dp, sp)
        self.started.append((copy, when))
        if when is None:
            copy.start()
        else:
            pl.when(when)(copy.start)

    def finish(self):
        for copy, when in self.started:
            if when is None:
                copy.wait_send()
            else:
                pl.when(when)(copy.wait_send)


def arrived(dst, recv):
    dp, sp, _, _ = place()
    remote(dst, dst, recv, recv, dp, sp).wait_recv()


SCALE = 1.0 / math.sqrt(SIZE)
FACTOR = SCALE * math.log2(math.e)
ANY = pl.BlockSpec(memory_space=pl.ANY)
DMA = pltpu.SemaphoreType.DMA


def lanes_of(i, width):
    return pl.ds(pl.multiple_of(i * width, width), width)


def forward_heads(c, qs, band, lb, bias, pb, rb, aa, an, dp):
    cols = lanes_of(c, SIZE)
    for h in range(2):
        head = 2 * c + h
        lanes = lanes_of(head, SIZE)
        q = qs[:, lanes]
        scores = []
        top = None
        for b in range(KB):
            k = band[0, b // 2, pl.ds(b % 2 * SIZE, SIZE), cols]
            s = lax.dot_general(k, q, NT, preferred_element_type=F32)
            s = s + bias[b * SIZE : (b + 1) * SIZE, :] + lb[head, b : b + 1, :]
            scores.append(s)
            t = jnp.max(s, axis=0, keepdims=True)
            top = t if top is None else jnp.maximum(top, t)
        total = jnp.zeros((1, TOK), F32)
        for b in range(KB):
            p = jnp.exp2((scores[b] - top) * FACTOR)
            total = total + jnp.sum(p, axis=0, keepdims=True)
            pb[head, b * SIZE : (b + 1) * SIZE, :] = p.astype(BF)
        v = band[1, :, :, cols].reshape(BAND, SIZE)
        out = lax.dot_general(v, pb[head], TN, preferred_element_type=F32)
        inverse = 1.0 / total
        rb[head] = jnp.broadcast_to(inverse, (8, TOK))
        out = out * inverse
        aa[dp, lanes, :] = out.astype(BF)
        an[:, lanes] = out.T.astype(BF)


def backward_heads(c, qs, band, pb, rb, aa, gt, dp):
    cols = lanes_of(c, SIZE)
    k = band[0, :, :, cols].reshape(BAND, SIZE)
    v = band[1, :, :, cols].reshape(BAND, SIZE)
    dk = jnp.zeros((BAND, SIZE), F32)
    dv = jnp.zeros((BAND, SIZE), F32)
    for h in range(2):
        head = 2 * c + h
        lanes = lanes_of(head, SIZE)
        inverse = rb[head, 0:1, :]
        g_t = gt[lanes, :].astype(F32)
        delta = jnp.sum(g_t * aa[dp, lanes, :].astype(F32), axis=0, keepdims=True) * inverse
        g_t = g_t * inverse
        g = g_t.T.astype(BF)
        grad_p = jnp.dot(v, g_t.astype(BF), preferred_element_type=F32)
        p = pb[head]
        grad_s = (p.astype(F32) * (grad_p - delta)).astype(BF)
        dq_t = lax.dot_general(k, grad_s, TN, preferred_element_type=F32)
        dk = dk + jnp.dot(grad_s, qs[:, lanes], preferred_element_type=F32)
        dv = dv + jnp.dot(p, g, preferred_element_type=F32)
        qs[:, lanes] = (dq_t * SCALE).T.astype(BF)
    band[0, :, :, cols] = (dk * SCALE).astype(BF).reshape(5, TOK, SIZE)
    band[1, :, :, cols] = dv.astype(BF).reshape(5, TOK, SIZE)


def layer_kernel(
    q_ref, k_ref, v_ref, lists_ref, len_ref, w_ref, d_ref,
    lo_ref, dq_ref, gkv_ref, gb_ref,
    band, lb, wb, db, qs, ds, bias, pb, rb, aa, an, gt, back, gw, rs, gsum,
    local, kv_send, kv_recv, w_send, w_recv, relay_send, pair_send, pair_recv, first_send, l_recv, d_recv,
    a_send, a_recv, a_relay, row_send, row_recv, z_send, z_recv, rs_send, rs_recv, g_send, g_recv,
):
    dp, sp, z, x = place()
    y, core = dp // 2, dp % 2
    other = dp_at(y, 1 - core)
    half = lanes_of(core, HALF)
    loads = [
        pltpu.make_async_copy(k_ref, band.at[0, 4], local.at[0]),
        pltpu.make_async_copy(v_ref, band.at[1, 4], local.at[1]),
        pltpu.make_async_copy(lists_ref.at[sp], lb.at[sp], local.at[2]),
        pltpu.make_async_copy(w_ref, wb.at[sp], local.at[3]),
        pltpu.make_async_copy(d_ref.at[:, lanes_of(dp, PART)], db.at[dp], local.at[4]),
        pltpu.make_async_copy(q_ref, qs, local.at[5]),
        pltpu.make_async_copy(d_ref, ds, local.at[6]),
    ]
    for copy in loads:
        copy.start()
    greet()
    kv_out, w_out, first_out = Sends(kv_send), Sends(w_send), Sends(first_send)
    own = (k_ref, v_ref)
    right, left = sp_at(z, x + 1), sp_at(z, x - 1)
    up, down = sp_at(z + 1, x), sp_at(z - 1, x)
    top, bottom = pl.ds(0, 64), pl.ds(64, 64)

    def kv(i, src, slot, to, when=None):
        kv_out.go(src, band.at[i, slot], kv_recv.at[i, slot], dp, to, when)

    def kv_here(i, slot):
        arrived(band.at[i, slot], kv_recv.at[i, slot])

    def weight(slot, rows, to):
        block = wb.at[slot, rows, half]
        w_out.go(block, block, w_recv.at[slot], dp, to)

    def weight_own(to):
        w_out.go(w_ref.at[:, half], wb.at[sp, :, half], w_recv.at[sp], dp, to)

    def weight_here(slot):
        arrived(wb.at[slot, :, half], w_recv.at[slot])

    def pair(slot):
        block = wb.at[slot, :, half]
        return remote(block, block, pair_send.at[slot], pair_recv.at[slot], other, sp)

    weight_own(right)
    weight_own(left)
    for i in (0, 1):
        kv(i, own[i], 0, up)
    for i in (0, 1):
        kv(i, own[i], 3, right, x < 3)
        kv(i, own[i], 1, left, x == 0)
    for r in range(1, 16):
        to = (sp + r) % 16
        first_out.go(lists_ref.at[to], lb.at[sp], l_recv, dp, to)
    weight_own(up)
    weight_own(down)
    for r in range(1, 8):
        to = (dp + r) % 8
        first_out.go(d_ref.at[:, lanes_of(to, PART)], db.at[dp], d_recv, to, sp)

    q_pos = sp * TOK + lax.broadcasted_iota(jnp.int32, (1, TOK), 1)
    begin = jnp.zeros((1, TOK), jnp.int32)
    start = jnp.int32(0)
    for i in range(16):
        begin = jnp.where(q_pos >= start, start, begin)
        start = start + len_ref[0, i]

    def mask(b, _):
        rows = pl.ds(pl.multiple_of(b * SIZE, SIZE), SIZE)
        k_pos = (sp - HALO) * TOK + b * SIZE + lax.broadcasted_iota(jnp.int32, (SIZE, TOK), 0)
        bias[rows, :] = jnp.where((k_pos <= q_pos) & (k_pos >= begin), 0.0, NEG)
        return 0

    lax.fori_loop(0, KB, mask, 0)

    whole = pl.ds(0, 128)
    a, b, c2 = left, right, sp_at(z, x + 2)
    weight_here(a)
    weight(a, top, right)
    weight(a, whole, up)
    weight(a, whole, down)
    weight_here(b)
    weight(b, bottom, left)
    weight(b, whole, up)
    weight(b, whole, down)
    pair(a).start()
    pair(b).start()
    for i in (0, 1):
        kv_here(i, 0)
        kv(i, band.at[i, 0], 3, right, x == 3)
        kv(i, band.at[i, 0], 1, left, x > 0)
    weight_here(c2)
    weight(c2, whole, up)
    weight(c2, whole, down)
    pair(c2).start()
    for i in (0, 1):
        kv_here(i, 3)
        kv(i, band.at[i, 3], 2, right, (x < 3) if i == 0 else (x == 2))
        kv_here(i, 1)
        kv(i, band.at[i, 1], 2, left, (x == 1) if i == 0 else (x > 0))
    for i in (0, 1):
        kv_here(i, 2)
    arrived(lb.at[pl.ds(0, 15)], l_recv)
    for copy in loads:
        copy.wait()

    def relay(i):
        above = i % 2
        slot = sp_at(z - 1 + 2 * above, x + i // 2)
        block = wb.at[slot, pl.ds(pl.multiple_of(above * 64, 64), 64), half]
        return slot, remote(block, block, relay_send.at[i], w_recv.at[slot], dp, sp_at(z + 1 - 2 * above, x))

    y_up, y_down, y_far = dp_at(y + 1, core), dp_at(y - 1, core), dp_at(y + 2, core)

    def forward(c, _):
        forward_heads(c, qs, band, lb, bias, pb, rb, aa, an, dp)
        rows = pl.ds(pl.multiple_of(c * TOK, TOK), TOK)
        block = aa.at[dp, rows]
        for i, to in enumerate((y_up, y_down, other)):
            remote(block, block, a_send.at[i], a_recv.at[dp], to, sp).start()
        slot, copy = relay(c)
        weight_here(slot)
        copy.start()
        pair(slot).start()
        return 0

    lax.fori_loop(0, 8, forward, 0)

    def far(i, _):
        slot = sp_at(z + 2, x + i)
        weight_here(slot)
        pair(slot).start()
        return 0

    lax.fori_loop(0, 4, far, 0)
    other_half = lanes_of(1 - core, HALF)

    def pairs(r, _):
        slot = (sp + r) % 16
        arrived(wb.at[slot, :, other_half], pair_recv.at[slot])
        return 0

    lax.fori_loop(1, 16, pairs, 0)

    def grad_attn(i, _):
        w = wb[pl.ds(2 * i, 2)].reshape(TOK, 3072)
        g = lax.dot_general(w, ds[...], NT, preferred_element_type=F32)
        gt[pl.ds(pl.multiple_of(i * TOK, TOK), TOK), :] = g.astype(BF)
        return 0

    lax.fori_loop(0, 8, grad_attn, 0)

    a_out = Sends(a_relay)

    def on(slot, rows, to):
        block = aa.at[slot, rows]
        a_out.go(block, block, a_recv.at[slot], to, sp)

    for slot, rows, to in ((y_down, pl.ds(0, 1024), y_up), (y_up, pl.ds(1024, 1024), y_down)):
        arrived(aa.at[slot], a_recv.at[slot])
        on(slot, rows, to)
        on(slot, pl.ds(0, 2048), other)
    kv_out.finish()

    def backward(c, _):
        backward_heads(c, qs, band, pb, rb, aa, gt, dp)
        cols = lanes_of(c, SIZE)
        for k in (2, 1, 3):
            remote(
                band.at[:, 4 - k, :, cols], back.at[k - 1, :, :, cols], row_send.at[k - 1], row_recv.at[k - 1, c], dp, sp_at(z, x - k)
            ).start()
        return 0

    lax.fori_loop(0, 8, backward, 0)
    dq_out = pltpu.make_async_copy(qs, dq_ref, local.at[7])
    dq_out.start()
    arrived(aa.at[y_far], a_recv.at[y_far])
    on(y_far, pl.ds(0, 2048), other)
    for r in range(4):
        slot = dp_at(y + r, 1 - core)
        arrived(aa.at[slot], a_recv.at[slot])
    arrived(db.at[pl.ds(0, 7)], d_recv)

    def weight_grad(t, _):
        j = (z + t) % 4
        rows = pl.ds(pl.multiple_of(j * 512, 512), 512)
        total = jnp.zeros((512, PART), F32)
        for e in range(8):
            total = total + jnp.dot(aa[e, rows, :], db[e], preferred_element_type=F32)
        gw[pl.ds(4 * j, 4)] = total.astype(BF).reshape(4, 128, PART)
        for i in range(4):
            to = 4 * j + (x + i) % 4

            @pl.when(to != sp)
            def _():
                remote(gw.at[to], rs.at[sp], rs_send, rs_recv, dp, to).start()

        return 0

    lax.fori_loop(0, 4, weight_grad, 0)

    keep = [jnp.where(x + k < 4, 1.0, 0.0).astype(F32) for k in (1, 2, 3)]

    def z_copy(c):
        cols = lanes_of(c, SIZE)
        return remote(band.at[:, 0, :, cols], back.at[3, :, :, cols], z_send, z_recv.at[c], dp, down)

    def row_sums(c, _):
        cols = lanes_of(c, SIZE)
        for k in range(3):
            arrived(back.at[k, :, :, cols], row_recv.at[k, c])
        below = band[:, 0, :, cols].astype(F32)
        here = band[:, 4, :, cols].astype(F32)
        for k in range(3):
            got = back[k, :, :, cols].astype(F32)
            here = here + got * keep[k]
            below = below + got * (1.0 - keep[k])
        band[:, 0, :, cols] = below.astype(BF)
        band[:, 4, :, cols] = here.astype(BF)
        z_copy(c).start()
        return 0

    lax.fori_loop(0, 8, row_sums, 0)

    def project(i, _):
        cols = lanes_of(i, 512)
        w = wb[:, :, cols].reshape(2048, 512)
        ds[:, cols] = jnp.dot(an[...], w, preferred_element_type=F32).astype(BF)
        return 0

    lax.fori_loop(0, 6, project, 0)
    lo_out = pltpu.make_async_copy(ds, lo_ref, local.at[8])
    lo_out.start()

    arrived(rs.at[pl.ds(0, 15)], rs_recv)
    total = gw[sp].astype(F32)
    for r in range(1, 16):
        total = total + rs[(sp + r) % 16].astype(F32)
    gsum[...] = total.astype(BF)
    g_out = Sends(g_send)
    for r in range(1, 8):
        g_out.go(gsum, gb_ref.at[dp], g_recv, (dp + r) % 8, sp)
    own_sum = pltpu.make_async_copy(gsum, gb_ref.at[dp], local.at[9])
    own_sum.start()

    def last(c, _):
        cols = lanes_of(c, SIZE)
        arrived(back.at[3, :, :, cols], z_recv.at[c])
        here = band[:, 4, :, cols].astype(F32) + back[3, :, :, cols].astype(F32)
        band[:, 4, :, cols] = here.astype(BF)
        return 0

    lax.fori_loop(0, 8, last, 0)
    gkv_out = pltpu.make_async_copy(band.at[:, 4], gkv_ref, local.at[10])
    gkv_out.start()

    w_out.finish()
    first_out.finish()
    a_out.finish()

    def relays(i, _):
        relay(i)[1].wait_send()
        return 0

    lax.fori_loop(0, 8, relays, 0)

    def pairs_sent(r, _):
        pair((sp + r) % 16).wait_send()
        return 0

    lax.fori_loop(1, 16, pairs_sent, 0)
    for i in range(3):
        remote(aa.at[dp], aa.at[dp], a_send.at[i], a_recv.at[dp], other, sp).wait_send()
    for k in range(3):
        remote(back.at[k], back.at[k], row_send.at[k], row_send.at[k], dp, left).wait_send()
    remote(back.at[3], back.at[3], z_send, z_send, dp, down).wait_send()
    remote(rs.at[pl.ds(0, 15)], rs.at[pl.ds(0, 15)], rs_send, rs_send, dp, left).wait_send()
    arrived(gb_ref.at[pl.ds(0, 7)], g_recv)
    g_out.finish()
    for copy in (dq_out, lo_out, own_sum, gkv_out):
        copy.wait()


def call_layer(q, k, v, lists, lengths, w, d):
    vmem = pltpu.VMEM
    return pl.pallas_call(
        layer_kernel,
        in_specs=[ANY] * 4 + [pl.BlockSpec(memory_space=pltpu.SMEM)] + [ANY] * 2,
        out_specs=[ANY] * 4,
        out_shape=[
            jax.ShapeDtypeStruct((TOK, 3072), BF),
            jax.ShapeDtypeStruct((TOK, 2048), BF),
            jax.ShapeDtypeStruct((2, TOK, 1024), BF),
            jax.ShapeDtypeStruct((8, 128, PART), BF),
        ],
        scratch_shapes=[
            vmem((2, 5, TOK, 1024), BF),
            vmem((16, 16, TOK), F32),
            vmem((16, 128, 3072), BF),
            vmem((8, TOK, PART), BF),
            vmem((TOK, 2048), BF),
            vmem((TOK, 3072), BF),
            vmem((BAND, TOK), F32),
            vmem((16, BAND, TOK), BF),
            vmem((16, 8, TOK), F32),
            vmem((8, 2048, TOK), BF),
            vmem((TOK, 2048), BF),
            vmem((2048, TOK), BF),
            vmem((4, 2, TOK, 1024), BF),
            vmem((16, 128, PART), BF),
            vmem((16, 128, PART), BF),
            vmem((128, PART), BF),
            DMA((11,)),
            DMA((16,)),
            DMA((2, 5)),
            DMA((12,)),
            DMA((16,)),
            DMA((8,)),
            DMA((16,)),
            DMA((16,)),
            DMA((22,)),
            DMA,
            DMA,
            DMA((3,)),
            DMA((8,)),
            DMA((5,)),
            DMA((3,)),
            DMA((3, 8)),
            DMA,
            DMA((8,)),
            DMA,
            DMA,
            DMA((7,)),
            DMA,
        ],
        compiler_params=pltpu.CompilerParams(collective_id=0, has_side_effects=True, vmem_limit_bytes=60 * 2**20),
        cost_estimate=pl.CostEstimate(flops=27 * 10**9, bytes_accessed=20 * 10**6, transcendentals=6 * 10**6),
    )(q, k, v, lists, lengths, w, d)


def per_device(queries, keys, values, key_blocks, block_counts, doc_lengths, out_weight, d_out):
    lists = list_terms(key_blocks[0, 0], block_counts[0, 0])
    layer_out, grad_q, grad_kv, grad_all = call_layer(
        queries[0], keys[0], values[0], lists, doc_lengths, out_weight, d_out[0]
    )
    grad_weight = grad_all.transpose(1, 0, 2).reshape(128, 3072).astype(F32)
    tokens = lax.axis_size("dp") * lax.axis_size("sp") * TOK
    grad_weight = grad_weight * (1.0 / math.sqrt(tokens))
    return (layer_out[None], grad_q[None], grad_kv[:1], grad_kv[1:], grad_weight)


def solution(mesh):
    in_specs = (
        P("dp", "sp", None),
        P("dp", "sp", None),
        P("dp", "sp", None),
        P("dp", "sp", None, None),
        P("dp", "sp", None),
        P("dp", None),
        P("sp", None),
        P("dp", "sp", None),
    )
    out_specs = (
        P("dp", "sp", None),
        P("dp", "sp", None),
        P("dp", "sp", None),
        P("dp", "sp", None),
        P("sp", None),
    )
    return jax.shard_map(per_device, mesh=mesh, in_specs=in_specs, out_specs=out_specs, check_vma=False)
```

time: 430 us -> 189 us (0.44)
  waiting for transfers between devices: 307 us -> 0 us
  Pallas kernels: 35.6 us -> 177 us
  starting transfers between devices: 18.2 us -> 0 us
  matrix products: 17.8 us -> 0 us
  local copies, waits for them, and re-layouts: 26.4 us -> 8.64 us
  between operations: 14.2 us -> 0.69 us
  other arithmetic: 9.07 us -> 1.55 us
    reduce_scatter x1 -> x0, waiting for transfers between devices: 144 us -> none  [per_device(): lax.psum_scatter(weight_part, 'sp', scatter_dimension=0, tiled=True)]
    pallas_call x2 -> x1, Pallas kernels: 35.6 us -> 177 us  [call_layer(): pl.pallas_call(layer_kernel, in_specs=[ANY] * 4 + [pl.BlockSpec(memory_sp...]
    ppermute x8 -> x0, waiting for transfers between devices: 93.1 us -> none  [the longest x4 93.1 us: per_device(): lax.ppermute(kv, 'sp', [(i, (i + s) % n) for i in range(n)])]
    psum x1 -> x0, waiting for transfers between devices: 56.8 us -> none  [per_device(): summed = lax.psum(shard_rows, 'dp').astype(F32)]
    dot_general x3 -> x0, matrix products: 17.8 us -> none  [the longest x1 6.73 us: per_device(): lax.dot_general(piece, grad_out, NT, preferred_element_type=F32).astype(BF)]
    unnamed x49 -> x9, local copies, waits for them, and re-layouts: 17.5 us -> 4.38 us
    all_gather x1 -> x0, waiting for transfers between devices: 12.7 us -> none  [per_device(): piece = lax.all_gather(out_weight, 'sp', axis=0, tiled=True)]
    ppermute x8 -> x0, starting transfers between devices: 12.3 us -> none  [the longest x4 7.43 us: per_device(): lax.ppermute(kv, 'sp', [(i, (i + s) % n) for i in range(n)])]
  transfers between devices with their start and end apart: 12 -> 0, of which waited for: 4 -> 0; matrix products, arithmetic and copies ran while one was open for 9% -> 0% of each run, Pallas kernels for 8% -> 0%
where the time goes in v3:
time: 189 us; the launch traced here: 188 us
  Pallas kernels  177 us (94%)
  local copies, waits for them, and re-layouts  8.64 us (5%)
    pallas_call x1, Pallas kernels, call_layer(): pl.pallas_call(layer_kernel, in_specs=[ANY] * 4 + [pl.BlockSpec(memory_sp...  177 us
    unnamed x9, local copies, waits for them, and re-layouts  4.38 us

profile of v3, /device:TPU:1, one launch (start us, length us, event | category | flops | bytes accessed | tf_op | source)
XLA Modules:
  0.0 188.1 jit_solution(7279483272819606121)
XLA Ops:
  0.6 0.7 iota_compare_fusion
  1.3 0.7 and_reduce_fusion
  2.0 0.1 copy.18
  2.1 0.2 copy.19
  2.3 0.3 broadcast_in_dim.24
  2.6 0.9 reshape.80.lists_ref
  3.5 177.2 %shard_map.119 = (bf16[256,3072]{1,0:T(8,128)(2,1)}, bf16[256,2048]{1,0:T(8,128)(2,1)}, bf16[2,256,1024]{2,1,0:T(8,128)(2,1)}, bf16[8,128,384]{2,1,0:T(8,128)(2,1)}) custom-call(bf16[256,2048]{1,0:T(8,128)(2,1)} %bitcast.20, bf16[256,1024]{1,0:T(8,128)(2,1)} %bitcast.21, bf16[256,1024]{1,0:T(8,128)(2,1)} %bitcast.22, f32[16,16,256]{2,1,0:T(8,128)} %reshape.80.lists_ref, ...), custom_call_target="tpu_custom_call" | custom-call | flops 27000000512 | bytes 20000000 | tf_op jit(solution)/shard_map/pallas_call | solution.py:447
  180.8 0.0 copy-start.2
  180.8 2.3 %fusion.2 = (bf16[1,256,1024]{2,1,0:T(8,128)(2,1)}, bf16[1,256,1024]{2,1,0:T(8,128)(2,1)}) fusion(bf16[2,256,1024]{2,1,0:T(8,128)(2,1)} %get-tuple-element.11), kind=kLoop, calls=%fused_computation.11 | loop fusion | bytes 2097152 | tf_op jit(solution)/shard_map/slice | solution.py:510
  183.1 0.0 copy-done.2
  183.1 0.2 multiply_bitcast_fusion
  183.3 0.5 copy.20
  183.7 0.0 copy-start
  183.7 1.6 copy.21
  185.4 0.0 copy-done
  185.4 0.0 copy-start.1
  185.4 1.1 copy.24
  186.5 0.6 copy-done.1
  187.1 1.0 copy.25
  (3 shorter events, 0.0 us)
Async XLA Ops:
  180.8 2.3 %copy-start.2 = (bf16[8,128,384]{2,1,0:T(8,128)(2,1)S(1)}, bf16[8,128,384]{2,1,0:T(8,128)(2,1)}, u32[]{:S(2)}) copy-start(bf16[8,128,384]{2,1,0:T(8,128)(2,1)} %get-tuple-element.12) | copy-start | bytes 2359300
  183.7 1.6 copy-start
  185.4 1.8 copy-start.1

commit v4 on v3

v4 whole, which is shorter than its diff:
```python
import math

import jax
import jax.numpy as jnp
from jax import lax
from jax.experimental import pallas as pl
from jax.experimental.pallas import tpu as pltpu
from jax.sharding import PartitionSpec as P

SIZE = 128
TOK = 256
HALO = 4
BAND = (HALO + 1) * TOK
KB = BAND // SIZE
NEG = -1e30
BF = jnp.bfloat16
F32 = jnp.float32
NT = (((1,), (1,)), ((), ()))
TN = (((0,), (0,)), ((), ()))


MESH = pl.DeviceIdType.MESH
PART = 384
HALF = 1536


def place():
    dp = lax.axis_index("dp")
    sp = lax.axis_index("sp")
    return dp, sp, sp // 4, sp % 4


def sp_at(z, x):
    return (z + 4) % 4 * 4 + (x + 4) % 4


def dp_at(y, core):
    return (y + 4) % 4 * 2 + core


def greet():
    dp, sp, _, _ = place()
    barrier = pltpu.get_barrier_semaphore()
    for r in range(1, 16):
        pl.semaphore_signal(barrier, inc=1, device_id=(dp, (sp + r) % 16), device_id_type=MESH)
    for r in range(1, 8):
        pl.semaphore_signal(barrier, inc=1, device_id=((dp + r) % 8, sp), device_id_type=MESH)
    pl.semaphore_wait(barrier, 22)


def remote(src, dst, send, recv, dp, sp):
    return pltpu.make_async_remote_copy(
        src_ref=src, dst_ref=dst, send_sem=send, recv_sem=recv, device_id=(dp, sp), device_id_type=MESH
    )


class Sends:
    def __init__(self, sems):
        self.sems = sems
        self.started = []

    def go(self, src, dst, recv, dp, sp, when=None):
        copy = remote(src, dst, self.sems.at[len(self.started)], recv, dp, sp)
        self.started.append((copy, when))
        if when is None:
            copy.start()
        else:
            pl.when(when)(copy.start)

    def finish(self):
        for copy, when in self.started:
            if when is None:
                copy.wait_send()
            else:
                pl.when(when)(copy.wait_send)


def arrived(dst, recv):
    dp, sp, _, _ = place()
    remote(dst, dst, recv, recv, dp, sp).wait_recv()


SCALE = 1.0 / math.sqrt(SIZE)
FACTOR = SCALE * math.log2(math.e)
ANY = pl.BlockSpec(memory_space=pl.ANY)
DMA = pltpu.SemaphoreType.DMA


def lanes_of(i, width):
    return pl.ds(pl.multiple_of(i * width, width), width)


def forward_heads(c, qs, band, lb, bias, pb, rb, aa, an, dp):
    cols = lanes_of(c, SIZE)
    for h in range(2):
        head = 2 * c + h
        lanes = lanes_of(head, SIZE)
        q = qs[:, lanes]
        scores = []
        top = None
        for b in range(KB):
            k = band[0, b // 2, pl.ds(b % 2 * SIZE, SIZE), cols]
            s = lax.dot_general(k, q, NT, preferred_element_type=F32)
            s = s + bias[b * SIZE : (b + 1) * SIZE, :] + lb[head, b : b + 1, :]
            scores.append(s)
            t = jnp.max(s, axis=0, keepdims=True)
            top = t if top is None else jnp.maximum(top, t)
        total = jnp.zeros((1, TOK), F32)
        for b in range(KB):
            p = jnp.exp2((scores[b] - top) * FACTOR)
            total = total + jnp.sum(p, axis=0, keepdims=True)
            pb[head, b * SIZE : (b + 1) * SIZE, :] = p.astype(BF)
        v = band[1, :, :, cols].reshape(BAND, SIZE)
        out = lax.dot_general(v, pb[head], TN, preferred_element_type=F32)
        inverse = 1.0 / total
        rb[head] = jnp.broadcast_to(inverse, (8, TOK))
        out = out * inverse
        aa[dp, lanes, :] = out.astype(BF)
        an[:, lanes] = out.T.astype(BF)


def backward_heads(c, qs, band, pb, rb, aa, gt, dp):
    cols = lanes_of(c, SIZE)
    k = band[0, :, :, cols].reshape(BAND, SIZE)
    v = band[1, :, :, cols].reshape(BAND, SIZE)
    dk = jnp.zeros((BAND, SIZE), F32)
    dv = jnp.zeros((BAND, SIZE), F32)
    for h in range(2):
        head = 2 * c + h
        lanes = lanes_of(head, SIZE)
        inverse = rb[head, 0:1, :]
        g_t = gt[lanes, :].astype(F32)
        delta = jnp.sum(g_t * aa[dp, lanes, :].astype(F32), axis=0, keepdims=True) * inverse
        g_t = g_t * inverse
        g = g_t.T.astype(BF)
        grad_p = jnp.dot(v, g_t.astype(BF), preferred_element_type=F32)
        p = pb[head]
        grad_s = (p.astype(F32) * (grad_p - delta)).astype(BF)
        dq_t = lax.dot_general(k, grad_s, TN, preferred_element_type=F32)
        dk = dk + jnp.dot(grad_s, qs[:, lanes], preferred_element_type=F32)
        dv = dv + jnp.dot(p, g, preferred_element_type=F32)
        qs[:, lanes] = (dq_t * SCALE).T.astype(BF)
    band[0, :, :, cols] = (dk * SCALE).astype(BF).reshape(5, TOK, SIZE)
    band[1, :, :, cols] = dv.astype(BF).reshape(5, TOK, SIZE)


def layer_kernel(
    q_ref, k_ref, v_ref, list_ref, cnt_ref, len_ref, w_ref, d_ref,
    lo_ref, dq_ref, gkv_ref, gkv_z_ref, gb_ref,
    band, raw, lb, wb, db, qs, ds, bias, pb, rb, aa, an, gt, back, gw, rs, rx, gsum,
    local, kv_send, kv_recv, w_send, w_recv, pair_send, pair_recv, first_send, l_recv, d_recv,
    a_send, a_recv, row_send, row_recv, z_send, z_recv, rs_send, rs_recv, g_send, g_recv,
):
    dp, sp, z, x = place()
    y, core = dp // 2, dp % 2
    other = dp_at(y, 1 - core)
    loads = [
        pltpu.make_async_copy(k_ref, band.at[0, 4], local.at[0]),
        pltpu.make_async_copy(v_ref, band.at[1, 4], local.at[1]),
        pltpu.make_async_copy(w_ref.at[:, lanes_of(core, HALF)], wb.at[sp, :, lanes_of(core, HALF)], local.at[3]),
        pltpu.make_async_copy(d_ref.at[:, lanes_of(dp, PART)], db.at[dp], local.at[4]),
        pltpu.make_async_copy(q_ref, qs, local.at[5]),
        pltpu.make_async_copy(d_ref, ds, local.at[6]),
    ]
    for copy in loads:
        copy.start()
    greet()
    first_out = Sends(first_send)
    up, down = sp_at(z + 1, x), sp_at(z - 1, x)
    y_up, y_down, y_far = dp_at(y + 1, core), dp_at(y - 1, core), dp_at(y + 2, core)

    def kv_up(j):
        cols = lanes_of(j, 256)
        return remote(band.at[:, 4, :, cols], band.at[:, 0, :, cols], kv_send.at[0], kv_recv.at[0, j], dp, up)

    def kv_row(k, j):
        cols = lanes_of(j, 256)
        src = band.at[:, jnp.where(x + k < 4, 4, 0), :, cols]
        return remote(src, band.at[:, 4 - k, :, cols], kv_send.at[k], kv_recv.at[4 - k, j], dp, sp_at(z, x + k))

    def kv_rows(j, mine):
        for k in (2, 1, 3):
            pl.when((x + k < 4) if mine else (x + k >= 4))(kv_row(k, j).start)

    def kv_here(slot, j):
        arrived(band.at[:, slot, :, lanes_of(j, 256)], kv_recv.at[slot, j])

    half, other_half = lanes_of(core, HALF), lanes_of(1 - core, HALF)
    w_out = Sends(w_send)

    def weight(slot, first, rows, to):
        block = wb.at[slot, pl.ds(first, rows), half]
        w_out.go(block, block, w_recv.at[slot], dp, to)

    def weight_here(slot):
        arrived(wb.at[slot, :, half], w_recv.at[slot])

    def weight_z(slot):
        weight(slot, 0, 128, up)
        weight(slot, 0, 128, down)

    def weight_relay(dx, above):
        slot = sp_at(z + 1 if above else z - 1, x + dx)
        weight_here(slot)
        if above:
            weight(slot, 0, 96, down)
        else:
            weight(slot, 96, 32, up)

    def weight_pair(row):
        block = wb.at[pl.ds(4 * row, 4), :, half]
        remote(block, block, pair_send, pair_recv.at[row], other, sp).start()

    def grad_attn(row):
        arrived(wb.at[pl.ds(4 * row, 4), :, other_half], pair_recv.at[row])

        def one(i, _):
            i = 2 * row + i
            w = wb[pl.ds(2 * i, 2)].reshape(TOK, 3072)
            g = lax.dot_general(w, ds[...], NT, preferred_element_type=F32)
            gt[pl.ds(pl.multiple_of(i * TOK, TOK), TOK), :] = g.astype(BF)
            return 0

        lax.fori_loop(0, 2, one, 0)

    def spread(slot, j, first, rows, send, to):
        block = aa.at[slot, pl.ds(j * 512 + first, rows)]
        remote(block, block, send, a_recv.at[slot, j], to, sp).start()

    def spread_here(slot, j):
        arrived(aa.at[slot, pl.ds(j * 512, 512)], a_recv.at[slot, j])

    def spread_own(j):
        for i, to in enumerate((y_up, y_down, other)):
            spread(dp, j, 0, 512, a_send.at[i], to)

    def spread_on(j):
        spread_here(y_down, j)
        spread(y_down, j, 0, 256, a_send.at[3], y_up)
        spread(y_down, j, 0, 512, a_send.at[4], other)
        spread_here(y_up, j)
        spread(y_up, j, 256, 256, a_send.at[5], y_down)
        spread(y_up, j, 0, 512, a_send.at[6], other)

    def spread_far(j):
        spread_here(y_far, j)
        spread(y_far, j, 0, 512, a_send.at[7], other)

    diagonal = lax.broadcasted_iota(jnp.int32, (32, 32), 0) == lax.broadcasted_iota(jnp.int32, (32, 32), 1)
    used = jnp.max(jnp.where(diagonal, cnt_ref[...], 0), axis=1, keepdims=True)
    raw[sp] = jnp.full((32, 128), -100, jnp.int32)
    raw[sp, :, 0:8] = jnp.where(lax.broadcasted_iota(jnp.int32, (32, 8), 1) < used, list_ref[...], -100)

    for copy in loads[:3]:
        copy.wait()
    for dx in (1, 3, 2):
        weight(sp, 0, 128, sp_at(z, x + dx))
    kv_up(0).start()
    weight_z(sp)
    for j in (1, 2, 3):
        kv_up(j).start()
    for r in range(1, 16):
        first_out.go(raw.at[sp], raw.at[sp], l_recv, dp, (sp + r) % 16)
    for r in (2, 6, 4, 1, 3, 5, 7):
        to = (dp + r) % 8
        first_out.go(d_ref.at[:, lanes_of(to, PART)], db.at[dp], d_recv, to, sp)

    q_pos = sp * TOK + lax.broadcasted_iota(jnp.int32, (1, TOK), 1)
    begin = jnp.zeros((1, TOK), jnp.int32)
    start = jnp.int32(0)
    for i in range(16):
        begin = jnp.where(q_pos >= start, start, begin)
        start = start + len_ref[0, i]

    def mask(b, _):
        rows = pl.ds(pl.multiple_of(b * SIZE, SIZE), SIZE)
        k_pos = (sp - HALO) * TOK + b * SIZE + lax.broadcasted_iota(jnp.int32, (SIZE, TOK), 0)
        bias[rows, :] = jnp.where((k_pos <= q_pos) & (k_pos >= begin), 0.0, NEG)
        return 0

    lax.fori_loop(0, KB, mask, 0)

    for dx in (1, 3):
        weight_here(sp_at(z, x + dx))
        weight_z(sp_at(z, x + dx))
    kv_rows(0, True)
    kv_here(0, 0)
    kv_rows(0, False)
    kv_rows(1, True)
    weight_here(sp_at(z, x + 2))
    weight_z(sp_at(z, x + 2))
    weight_pair(z)
    for j in (1, 2):
        kv_here(0, j)
        kv_rows(j, False)
        kv_rows(j + 1, True)
    weight_relay(0, True)
    weight_relay(0, False)
    kv_here(0, 3)
    kv_rows(3, False)
    arrived(raw.at[pl.ds(0, 15)], l_recv)

    def list_terms(h, _):
        ids = 2 * sp - 2 * HALO + lax.broadcasted_iota(jnp.int32, (16, 128), 0)
        for i in range(2):
            found = jnp.where(raw[h, pl.ds(2 * sp + i, 1), :] == ids, 0.0, NEG)
            found = jnp.max(found, axis=1, keepdims=True)
            lb[h, :, i * SIZE : (i + 1) * SIZE] = jnp.broadcast_to(found, (16, SIZE))
        return 0

    lax.fori_loop(0, 16, list_terms, 0)
    for copy in loads[3:]:
        copy.wait()
    grad_attn(z)

    def forward(c, _):
        forward_heads(c, qs, band, lb, bias, pb, rb, aa, an, dp)
        return 0

    for j in range(4):
        for slot in (3, 1, 2):
            kv_here(slot, j)
        lax.fori_loop(2 * j, 2 * j + 2, forward, 0)
        spread_own(j)
        if j < 3:
            dx = (1, 3, 2)[j]
            weight_relay(dx, True)
            weight_relay(dx, False)
        if j > 0:
            spread_on(j - 1)
    row_above, row_below, row_far = (z + 1) % 4, (z + 3) % 4, (z + 2) % 4
    weight_pair(row_above)
    weight_pair(row_below)
    grad_attn(row_above)
    grad_attn(row_below)
    spread_on(3)
    for i in range(4):
        weight_here(4 * row_far + i)
    weight_pair(row_far)
    for j in range(3):
        spread_far(j)
    grad_attn(row_far)
    for k in range(4):
        remote(band.at[:, 0], band.at[:, 0], kv_send.at[k], kv_send.at[k], dp, up).wait_send()

    def backward(c, _):
        backward_heads(c, qs, band, pb, rb, aa, gt, dp)
        cols = lanes_of(c, SIZE)
        for k in (2, 1, 3):
            remote(
                band.at[:, 4 - k, :, cols], back.at[k - 1, :, :, cols], row_send.at[k - 1], row_recv.at[k - 1, c], dp, sp_at(z, x - k)
            ).start()
        return 0

    lax.fori_loop(0, 8, backward, 0)
    dq_out = pltpu.make_async_copy(qs, dq_ref, local.at[7])
    dq_out.start()
    spread_far(3)
    for r in range(4):
        for j in range(4):
            spread_here(dp_at(y + r, 1 - core), j)
    arrived(db.at[pl.ds(0, 7)], d_recv)

    def weight_grad(t, _):
        j = (z + 1 + t) % 4
        rows = pl.ds(pl.multiple_of(j * 512, 512), 512)
        total = jnp.zeros((512, PART), F32)
        for e in range(8):
            total = total + jnp.dot(aa[e, rows, :], db[e], preferred_element_type=F32)
        gw[pl.ds(4 * j, 4)] = total.astype(BF).reshape(4, 128, PART)

        @pl.when(t < 3)
        def _():
            remote(gw.at[pl.ds(4 * j, 4)], rs.at[pl.ds(4 * t, 4)], rs_send.at[0], rs_recv.at[0], dp, sp_at(j, x)).start()

        return 0

    lax.fori_loop(0, 4, weight_grad, 0)

    keep = [jnp.where(x + k < 4, 1.0, 0.0).astype(F32) for k in (1, 2, 3)]

    def z_copy(c):
        cols = lanes_of(c, SIZE)
        return remote(band.at[:, 0, :, cols], gkv_z_ref.at[:, :, cols], z_send, z_recv, dp, down)

    def row_sums(c, _):
        cols = lanes_of(c, SIZE)
        for k in range(3):
            arrived(back.at[k, :, :, cols], row_recv.at[k, c])
        below = band[:, 0, :, cols].astype(F32)
        here = band[:, 4, :, cols].astype(F32)
        for k in range(3):
            got = back[k, :, :, cols].astype(F32)
            here = here + got * keep[k]
            below = below + got * (1.0 - keep[k])
        band[:, 0, :, cols] = below.astype(BF)
        band[:, 4, :, cols] = here.astype(BF)
        z_copy(c).start()
        return 0


    def project(i, _):
        cols = lanes_of(i, 512)
        w = wb[:, :, cols].reshape(2048, 512)
        ds[:, cols] = jnp.dot(an[...], w, preferred_element_type=F32).astype(BF)
        return 0

    lax.fori_loop(0, 6, project, 0)
    lo_out = pltpu.make_async_copy(ds, lo_ref, local.at[8])
    lo_out.start()

    lax.fori_loop(0, 3, row_sums, 0)
    arrived(rs.at[pl.ds(0, 12)], rs_recv.at[0])

    def z_sums(i, _):
        total = gw[4 * z + i].astype(F32)
        for t in range(3):
            total = total + rs[4 * t + i].astype(F32)
        rs[12 + i] = total.astype(BF)

        @pl.when(i != x)
        def _():
            k = (x - i + 4) % 4 - 1
            remote(rs.at[12 + i], rx.at[k], rs_send.at[1], rs_recv.at[1], dp, sp_at(z, i)).start()

        return 0

    lax.fori_loop(0, 4, z_sums, 0)
    lax.fori_loop(3, 5, row_sums, 0)
    arrived(rx, rs_recv.at[1])
    total = rs[12 + x].astype(F32)
    for r in range(3):
        total = total + rx[r].astype(F32)
    gsum[...] = total.astype(BF)
    g_out = Sends(g_send)
    for r in range(1, 8):
        g_out.go(gsum, gb_ref.at[:, lanes_of(dp, PART)], g_recv, (dp + r) % 8, sp)
    own_sum = pltpu.make_async_copy(gsum, gb_ref.at[:, lanes_of(dp, PART)], local.at[9])
    own_sum.start()

    lax.fori_loop(5, 8, row_sums, 0)
    arrived(gkv_z_ref, z_recv)
    gkv_out = pltpu.make_async_copy(band.at[:, 4], gkv_ref, local.at[10])
    gkv_out.start()

    first_out.finish()
    w_out.finish()
    some = wb.at[:, :, half]
    remote(some, some, pair_send, pair_send, other, sp).wait_send()
    for i in range(8):
        some = aa.at[dp, pl.ds(0, 1024 if i in (3, 5) else 2048)]
        remote(some, some, a_send.at[i], a_send.at[i], other, sp).wait_send()
    for k in range(3):
        remote(back.at[k], back.at[k], row_send.at[k], row_send.at[k], dp, up).wait_send()
    remote(gkv_z_ref, gkv_z_ref, z_send, z_send, dp, down).wait_send()
    remote(rs.at[pl.ds(0, 12)], rs.at[pl.ds(0, 12)], rs_send.at[0], rs_send.at[0], dp, up).wait_send()
    remote(rx, rx, rs_send.at[1], rs_send.at[1], dp, up).wait_send()
    arrived(gb_ref.at[:, pl.ds(0, 7 * PART)], g_recv)
    g_out.finish()
    for copy in (dq_out, lo_out, own_sum, gkv_out):
        copy.wait()


def call_layer(q, k, v, lists, counts, lengths, w, d):
    vmem = pltpu.VMEM
    return pl.pallas_call(
        layer_kernel,
        in_specs=[ANY] * 3
        + [pl.BlockSpec(memory_space=vmem)] * 2
        + [pl.BlockSpec(memory_space=pltpu.SMEM)]
        + [ANY] * 2,
        out_specs=[ANY] * 5,
        out_shape=[
            jax.ShapeDtypeStruct((TOK, 3072), BF),
            jax.ShapeDtypeStruct((TOK, 2048), BF),
            jax.ShapeDtypeStruct((2, TOK, 1024), BF),
            jax.ShapeDtypeStruct((2, TOK, 1024), BF),
            jax.ShapeDtypeStruct((128, 3072), BF),
        ],
        scratch_shapes=[
            vmem((2, 5, TOK, 1024), BF),
            vmem((16, 32, 128), jnp.int32),
            vmem((16, 16, TOK), F32),
            vmem((16, 128, 3072), BF),
            vmem((8, TOK, PART), BF),
            vmem((TOK, 2048), BF),
            vmem((TOK, 3072), BF),
            vmem((BAND, TOK), F32),
            vmem((16, BAND, TOK), BF),
            vmem((16, 8, TOK), F32),
            vmem((8, 2048, TOK), BF),
            vmem((TOK, 2048), BF),
            vmem((2048, TOK), BF),
            vmem((3, 2, TOK, 1024), BF),
            vmem((16, 128, PART), BF),
            vmem((16, 128, PART), BF),
            vmem((3, 128, PART), BF),
            vmem((128, PART), BF),
            DMA((11,)),
            DMA((4,)),
            DMA((4, 4)),
            DMA((19,)),
            DMA((16,)),
            DMA,
            DMA((4,)),
            DMA((22,)),
            DMA,
            DMA,
            DMA((8,)),
            DMA((8, 4)),
            DMA((3,)),
            DMA((3, 8)),
            DMA,
            DMA,
            DMA((2,)),
            DMA((2,)),
            DMA((7,)),
            DMA,
        ],
        compiler_params=pltpu.CompilerParams(collective_id=0, has_side_effects=True, vmem_limit_bytes=60 * 2**20),
        cost_estimate=pl.CostEstimate(flops=27 * 10**9, bytes_accessed=20 * 10**6, transcendentals=6 * 10**6),
    )(q, k, v, lists, counts, lengths, w, d)


def per_device(queries, keys, values, key_blocks, block_counts, doc_lengths, out_weight, d_out):
    layer_out, grad_q, grad_kv, more_kv, grad_all = call_layer(
        queries[0], keys[0], values[0], key_blocks[0, 0], block_counts[0], doc_lengths, out_weight, d_out[0]
    )
    grad_kv = (grad_kv.astype(F32) + more_kv.astype(F32)).astype(BF)
    grad_weight = grad_all.astype(F32)
    tokens = lax.axis_size("dp") * lax.axis_size("sp") * TOK
    grad_weight = grad_weight * (1.0 / math.sqrt(tokens))
    return (layer_out[None], grad_q[None], grad_kv[:1], grad_kv[1:], grad_weight)


def solution(mesh):
    in_specs = (
        P("dp", "sp", None),
        P("dp", "sp", None),
        P("dp", "sp", None),
        P("dp", "sp", None, None),
        P("dp", "sp", None),
        P("dp", None),
        P("sp", None),
        P("dp", "sp", None),
    )
    out_specs = (
        P("dp", "sp", None),
        P("dp", "sp", None),
        P("dp", "sp", None),
        P("dp", "sp", None),
        P("sp", None),
    )
    return jax.shard_map(per_device, mesh=mesh, in_specs=in_specs, out_specs=out_specs, check_vma=False)
```

time: 189 us -> 169 us (0.89)
  Pallas kernels: 177 us -> 159 us
  local copies, waits for them, and re-layouts: 8.64 us -> 5.61 us
    pallas_call x1, Pallas kernels: 177 us -> 159 us  [call_layer(): pl.pallas_call(layer_kernel, in_specs=[ANY] * 3 + [pl.BlockSpec(memory_sp...]
    convert_element_type x0 -> x1, other arithmetic: none -> 1.93 us  [per_device(): grad_kv = (grad_kv.astype(F32) + more_kv.astype(F32)).astype(BF)]
where the time goes in v4:
time: 169 us
  Pallas kernels  159 us (94%)
  local copies, waits for them, and re-layouts  5.61 us (3%)
  other arithmetic  3.25 us (2%)
    pallas_call x1, Pallas kernels, call_layer(): pl.pallas_call(layer_kernel, in_specs=[ANY] * 3 + [pl.BlockSpec(memory_sp...  159 us
    unnamed x9, local copies, waits for them, and re-layouts  4.58 us

profile of v4, /device:TPU:1, one launch (start us, length us, event | category | flops | bytes accessed | tf_op | source)
XLA Modules:
  0.0 168.8 jit_solution(438316932589486499)
XLA Ops:
  0.6 1.4 copy.13
  2.0 159.3 %shard_map.119 = (bf16[256,3072]{1,0:T(8,128)(2,1)}, bf16[256,2048]{1,0:T(8,128)(2,1)}, bf16[2,256,1024]{2,1,0:T(8,128)(2,1)}, bf16[2,256,1024]{2,1,0:T(8,128)(2,1)}, bf16[128,3072]{1,0:T(8,128)(2,1)}) custom-call(bf16[256,2048]{1,0:T(8,128)(2,1)} %bitcast.12, bf16[256,1024]{1,0:T(8,128)(2,1)} %bitcast.13, bf16[256,1024]{1,0:T(8,128)(2,1)} %bitcast.14, ...), custom_call_target="tpu_custom_call" | custom-call | flops 27000000512 | bytes 20000000 | tf_op jit(solution)/shard_map/pallas_call | solution.py:466
  161.3 1.9 %add_convert_fusion = bf16[2,256,1024]{2,1,0:T(8,128)(2,1)S(1)} fusion(bf16[2,256,1024]{2,1,0:T(8,128)(2,1)} %get-tuple-element.13, bf16[2,256,1024]{2,1,0:T(8,128)(2,1)} %get-tuple-element.12), kind=kLoop, calls=%fused_computation | loop fusion | flops 2097152 | bytes 3145728 | tf_op jit(solution)/shard_map/convert_element_type | solution.py:529
  163.2 0.0 copy-start.2
  163.2 1.0 fusion
  164.3 0.0 copy-start
  164.3 0.4 copy-done.2
  164.7 1.3 convert_multiply_fusion
  166.0 0.0 copy-done
  166.0 0.0 copy-start.1
  166.0 1.1 copy.16
  167.2 0.6 copy-done.1
  167.8 1.0 copy.17
Async XLA Ops:
  163.2 1.5 copy-start.2
  164.3 1.8 %copy-start = (bf16[256,3072]{1,0:T(8,128)(2,1)S(1)}, bf16[256,3072]{1,0:T(8,128)(2,1)}, u32[]{:S(2)}) copy-start(bf16[256,3072]{1,0:T(8,128)(2,1)} %get-tuple-element.10) | copy-start | bytes 4718596
  166.0 1.8 %copy-start.1 = (bf16[256,2048]{1,0:T(8,128)(2,1)S(1)}, bf16[256,2048]{1,0:T(8,128)(2,1)}, u32[]{:S(2)}) copy-start(bf16[256,2048]{1,0:T(8,128)(2,1)} %get-tuple-element.11) | copy-start | bytes 3145732

commit v5 on v4

--- a/solution.py
+++ b/solution.py
@@ -148,7 +148,7 @@
     q_ref, k_ref, v_ref, list_ref, cnt_ref, len_ref, w_ref, d_ref,
     lo_ref, dq_ref, gkv_ref, gkv_z_ref, gb_ref,
     band, raw, lb, wb, db, qs, ds, bias, pb, rb, aa, an, gt, back, gw, rs, rx, gsum,
-    local, kv_send, kv_recv, w_send, w_recv, pair_send, pair_recv, first_send, l_recv, d_recv,
+    local, kv_send, kv_recv, w_send, w_recv, q_recv, pair_send, pair_recv, first_send, l_recv, d_recv,
     a_send, a_recv, row_send, row_recv, z_send, z_recv, rs_send, rs_recv, g_send, g_recv,
 ):
     dp, sp, z, x = place()
@@ -165,18 +165,22 @@
     for copy in loads:
         copy.start()
     greet()
+    def chunks(row):
+        return [(row + i) % 4 for i in (0, 1, 3, 2)]
+
+    order = chunks(z)
     first_out = Sends(first_send)
     up, down = sp_at(z + 1, x), sp_at(z - 1, x)
     y_up, y_down, y_far = dp_at(y + 1, core), dp_at(y - 1, core), dp_at(y + 2, core)
 
     def kv_up(j):
         cols = lanes_of(j, 256)
-        return remote(band.at[:, 4, :, cols], band.at[:, 0, :, cols], kv_send.at[0], kv_recv.at[0, j], dp, up)
+        return remote(band.at[:, 4, :, cols], band.at[:, 0, :, cols], kv_send.at[0, j], kv_recv.at[0, j], dp, up)
 
     def kv_row(k, j):
         cols = lanes_of(j, 256)
         src = band.at[:, jnp.where(x + k < 4, 4, 0), :, cols]
-        return remote(src, band.at[:, 4 - k, :, cols], kv_send.at[k], kv_recv.at[4 - k, j], dp, sp_at(z, x + k))
+        return remote(src, band.at[:, 4 - k, :, cols], kv_send.at[k, j], kv_recv.at[4 - k, j], dp, sp_at(z, x + k))
 
     def kv_rows(j, mine):
         for k in (2, 1, 3):
@@ -194,6 +198,18 @@
 
     def weight_here(slot):
         arrived(wb.at[slot, :, half], w_recv.at[slot])
+
+    def weight_quarter(slot, recv, to_dp, to_sp):
+        block = wb.at[slot, pl.ds(pl.multiple_of(32 * y, 32), 32), half]
+        w_out.go(block, block, recv, to_dp, to_sp)
+
+    def weight_quarter_here(slot):
+        arrived(wb.at[slot, pl.ds(0, 32), half], q_recv.at[slot])
+        for dy in (1, 3, 2):
+            weight_quarter(slot, w_recv.at[slot], dp_at(y + dy, core), sp)
+
+    def weight_rest_here(slot):
+        arrived(wb.at[slot, pl.ds(0, 96), half], w_recv.at[slot])
 
     def weight_z(slot):
         weight(slot, 0, 128, up)
@@ -254,16 +270,14 @@
     for copy in loads[:3]:
         copy.wait()
     for dx in (1, 3, 2):
-        weight(sp, 0, 128, sp_at(z, x + dx))
-    kv_up(0).start()
+        weight_quarter(sp, q_recv.at[sp], dp, sp_at(z, x + dx))
+    first, *others = chunks(z + 1)
+    kv_up(first).start()
     weight_z(sp)
-    for j in (1, 2, 3):
+    for j in others:
         kv_up(j).start()
     for r in range(1, 16):
         first_out.go(raw.at[sp], raw.at[sp], l_recv, dp, (sp + r) % 16)
-    for r in (2, 6, 4, 1, 3, 5, 7):
-        to = (dp + r) % 8
-        first_out.go(d_ref.at[:, lanes_of(to, PART)], db.at[dp], d_recv, to, sp)
 
     q_pos = sp * TOK + lax.broadcasted_iota(jnp.int32, (1, TOK), 1)
     begin = jnp.zeros((1, TOK), jnp.int32)
@@ -280,24 +294,22 @@
 
     lax.fori_loop(0, KB, mask, 0)
 
-    for dx in (1, 3):
-        weight_here(sp_at(z, x + dx))
+    for dx in (1, 3, 2):
+        weight_quarter_here(sp_at(z, x + dx))
+    kv_rows(order[0], True)
+    kv_rows(order[1], True)
+    kv_here(0, order[0])
+    kv_rows(order[0], False)
+    for dx in (1, 3, 2):
+        weight_rest_here(sp_at(z, x + dx))
         weight_z(sp_at(z, x + dx))
-    kv_rows(0, True)
-    kv_here(0, 0)
-    kv_rows(0, False)
-    kv_rows(1, True)
-    weight_here(sp_at(z, x + 2))
-    weight_z(sp_at(z, x + 2))
     weight_pair(z)
-    for j in (1, 2):
-        kv_here(0, j)
-        kv_rows(j, False)
-        kv_rows(j + 1, True)
-    weight_relay(0, True)
-    weight_relay(0, False)
-    kv_here(0, 3)
-    kv_rows(3, False)
+    for r in (2, 6, 4, 1, 3, 5, 7):
+        to = (dp + r) % 8
+        first_out.go(d_ref.at[:, lanes_of(to, PART)], db.at[dp], d_recv, to, sp)
+    kv_here(0, order[1])
+    kv_rows(order[1], False)
+    kv_rows(order[2], True)
     arrived(raw.at[pl.ds(0, 15)], l_recv)
 
     def list_terms(h, _):
@@ -311,93 +323,140 @@
     lax.fori_loop(0, 16, list_terms, 0)
     for copy in loads[3:]:
         copy.wait()
+    kv_here(0, order[2])
+    kv_rows(order[2], False)
+    kv_rows(order[3], True)
     grad_attn(z)
 
     def forward(c, _):
         forward_heads(c, qs, band, lb, bias, pb, rb, aa, an, dp)
         return 0
 
-    for j in range(4):
-        for slot in (3, 1, 2):
-            kv_here(slot, j)
-        lax.fori_loop(2 * j, 2 * j + 2, forward, 0)
-        spread_own(j)
-        if j < 3:
-            dx = (1, 3, 2)[j]
-            weight_relay(dx, True)
-            weight_relay(dx, False)
-        if j > 0:
-            spread_on(j - 1)
-    row_above, row_below, row_far = (z + 1) % 4, (z + 3) % 4, (z + 2) % 4
-    weight_pair(row_above)
-    weight_pair(row_below)
-    grad_attn(row_above)
-    grad_attn(row_below)
-    spread_on(3)
-    for i in range(4):
-        weight_here(4 * row_far + i)
-    weight_pair(row_far)
-    for j in range(3):
-        spread_far(j)
-    grad_attn(row_far)
-    for k in range(4):
-        remote(band.at[:, 0], band.at[:, 0], kv_send.at[k], kv_send.at[k], dp, up).wait_send()
-
     def backward(c, _):
         backward_heads(c, qs, band, pb, rb, aa, gt, dp)
-        cols = lanes_of(c, SIZE)
+        return 0
+
+    def backward_chunk(j):
+        cols = lanes_of(j, 256)
+        for k in range(4):
+            remote(band.at[:, 0, :, cols], band.at[:, 0, :, cols], kv_send.at[k, j], kv_send.at[k, j], dp, up).wait_send()
+        lax.fori_loop(2 * j, 2 * j + 2, backward, 0)
+
+    def give_back(j):
+        cols = lanes_of(j, 256)
         for k in (2, 1, 3):
             remote(
-                band.at[:, 4 - k, :, cols], back.at[k - 1, :, :, cols], row_send.at[k - 1], row_recv.at[k - 1, c], dp, sp_at(z, x - k)
+                band.at[:, 4 - k, :, cols], back.at[k - 1, :, :, cols], row_send.at[k - 1], row_recv.at[k - 1, j], dp, sp_at(z, x - k)
             ).start()
-        return 0
-
-    lax.fori_loop(0, 8, backward, 0)
-    dq_out = pltpu.make_async_copy(qs, dq_ref, local.at[7])
-    dq_out.start()
-    spread_far(3)
-    for r in range(4):
-        for j in range(4):
+
+    def spread_in(j):
+        for r in range(4):
             spread_here(dp_at(y + r, 1 - core), j)
-    arrived(db.at[pl.ds(0, 7)], d_recv)
-
-    def weight_grad(t, _):
-        j = (z + 1 + t) % 4
+
+    def weight_grad(j):
         rows = pl.ds(pl.multiple_of(j * 512, 512), 512)
         total = jnp.zeros((512, PART), F32)
         for e in range(8):
             total = total + jnp.dot(aa[e, rows, :], db[e], preferred_element_type=F32)
         gw[pl.ds(4 * j, 4)] = total.astype(BF).reshape(4, 128, PART)
 
-        @pl.when(t < 3)
-        def _():
-            remote(gw.at[pl.ds(4 * j, 4)], rs.at[pl.ds(4 * t, 4)], rs_send.at[0], rs_recv.at[0], dp, sp_at(j, x)).start()
-
-        return 0
-
-    lax.fori_loop(0, 4, weight_grad, 0)
-
+    def scatter_z(j):
+        k = (z - j + 4) % 4 - 1
+        remote(gw.at[pl.ds(4 * j, 4)], rs.at[pl.ds(4 * k, 4)], rs_send.at[0], rs_recv.at[0], dp, sp_at(j, x)).start()
+
+    def kv_chunk(j):
+        for slot in (3, 1, 2):
+            kv_here(slot, j)
+
+    def forward_chunk(j):
+        lax.fori_loop(2 * j, 2 * j + 2, forward, 0)
+        spread_own(j)
+
+    own_row, row_above, row_below, row_far = order
+
+    kv_chunk(own_row)
+    forward_chunk(own_row)
+    kv_here(0, order[3])
+    kv_rows(order[3], False)
+    weight_relay(0, True)
+    weight_relay(1, True)
+    weight_relay(0, False)
+    weight_relay(1, False)
+    backward_chunk(own_row)
+    weight_relay(3, True)
+    weight_relay(3, False)
+    spread_on(own_row)
+
+    kv_chunk(row_above)
+    forward_chunk(row_above)
+    weight_relay(2, True)
+    weight_pair(row_above)
+    weight_relay(2, False)
+    weight_pair(row_below)
+    grad_attn(row_above)
+    backward_chunk(row_above)
+    spread_on(row_above)
+    spread_far(own_row)
+
+    kv_chunk(row_below)
+    give_back(own_row)
+    forward_chunk(row_below)
+    grad_attn(row_below)
+    backward_chunk(row_below)
+    spread_on(row_below)
+    spread_far(row_above)
+    arrived(db.at[pl.ds(0, 7)], d_recv)
+    spread_in(own_row)
+    weight_grad(own_row)
+    for i in range(4):
+        weight_here(4 * row_far + i)
+    weight_pair(row_far)
+
+    kv_chunk(row_far)
+    give_back(row_above)
+    give_back(row_below)
+    forward_chunk(row_far)
+    grad_attn(row_far)
+    backward_chunk(row_far)
+    give_back(row_far)
+    dq_out = pltpu.make_async_copy(qs, dq_ref, local.at[7])
+    dq_out.start()
+    spread_on(row_far)
+    spread_far(row_below)
+    spread_in(row_above)
+    weight_grad(row_above)
+    scatter_z(row_above)
+    spread_far(row_far)
+    spread_in(row_below)
+    weight_grad(row_below)
+    scatter_z(row_below)
+    spread_in(row_far)
+    weight_grad(row_far)
+    scatter_z(row_far)
     keep = [jnp.where(x + k < 4, 1.0, 0.0).astype(F32) for k in (1, 2, 3)]
 
-    def z_copy(c):
-        cols = lanes_of(c, SIZE)
+    def z_copy(j):
+        cols = lanes_of(j, 256)
         return remote(band.at[:, 0, :, cols], gkv_z_ref.at[:, :, cols], z_send, z_recv, dp, down)
 
-    def row_sums(c, _):
-        cols = lanes_of(c, SIZE)
+    def row_sums(j):
         for k in range(3):
-            arrived(back.at[k, :, :, cols], row_recv.at[k, c])
-        below = band[:, 0, :, cols].astype(F32)
-        here = band[:, 4, :, cols].astype(F32)
-        for k in range(3):
-            got = back[k, :, :, cols].astype(F32)
-            here = here + got * keep[k]
-            below = below + got * (1.0 - keep[k])
-        band[:, 0, :, cols] = below.astype(BF)
-        band[:, 4, :, cols] = here.astype(BF)
-        z_copy(c).start()
-        return 0
-
+            arrived(back.at[k, :, :, lanes_of(j, 256)], row_recv.at[k, j])
+
+        def one(c, _):
+            cols = lanes_of(c, SIZE)
+            below = band[:, 0, :, cols].astype(F32)
+            here = band[:, 4, :, cols].astype(F32)
+            for k in range(3):
+                got = back[k, :, :, cols].astype(F32)
+                here = here + got * keep[k]
+                below = below + got * (1.0 - keep[k])
+            band[:, 0, :, cols] = below.astype(BF)
+            band[:, 4, :, cols] = here.astype(BF)
+            return 0
+
+        lax.fori_loop(2 * j, 2 * j + 2, one, 0)
+        z_copy(j).start()
 
     def project(i, _):
         cols = lanes_of(i, 512)
@@ -409,7 +468,7 @@
     lo_out = pltpu.make_async_copy(ds, lo_ref, local.at[8])
     lo_out.start()
 
-    lax.fori_loop(0, 3, row_sums, 0)
+    row_sums(own_row)
     arrived(rs.at[pl.ds(0, 12)], rs_recv.at[0])
 
     def z_sums(i, _):
@@ -426,7 +485,7 @@
         return 0
 
     lax.fori_loop(0, 4, z_sums, 0)
-    lax.fori_loop(3, 5, row_sums, 0)
+    row_sums(row_above)
     arrived(rx, rs_recv.at[1])
     total = rs[12 + x].astype(F32)
     for r in range(3):
@@ -438,7 +497,8 @@
     own_sum = pltpu.make_async_copy(gsum, gb_ref.at[:, lanes_of(dp, PART)], local.at[9])
     own_sum.start()
 
-    lax.fori_loop(5, 8, row_sums, 0)
+    row_sums(row_below)
+    row_sums(row_far)
     arrived(gkv_z_ref, z_recv)
     gkv_out = pltpu.make_async_copy(band.at[:, 4], gkv_ref, local.at[10])
     gkv_out.start()
@@ -497,9 +557,10 @@
             vmem((3, 128, PART), BF),
             vmem((128, PART), BF),
             DMA((11,)),
-            DMA((4,)),
             DMA((4, 4)),
-            DMA((19,)),
+            DMA((4, 4)),
+            DMA((28,)),
+            DMA((16,)),
             DMA((16,)),
             DMA,
             DMA((4,)),
@@ -509,7 +570,7 @@
             DMA((8,)),
             DMA((8, 4)),
             DMA((3,)),
-            DMA((3, 8)),
+            DMA((3, 4)),
             DMA,
             DMA,
             DMA((2,)),

time: 169 us -> 155 us (0.917); the launches traced: 169 us -> 153 us
  Pallas kernels: 159 us -> 143 us
    pallas_call x1, Pallas kernels: 159 us -> 143 us  [call_layer(): pl.pallas_call(layer_kernel, in_specs=[ANY] * 3 + [pl.BlockSpec(memory_sp...]
where the time goes in v5:
time: 155 us; the launch traced here: 153 us
  Pallas kernels  143 us (92%)
  local copies, waits for them, and re-layouts  5.61 us (4%)
  other arithmetic  3.25 us (2%)
    pallas_call x1, Pallas kernels, call_layer(): pl.pallas_call(layer_kernel, in_specs=[ANY] * 3 + [pl.BlockSpec(memory_sp...  143 us
    unnamed x9, local copies, waits for them, and re-layouts  4.58 us

profile of v5, /device:TPU:1, one launch (start us, length us, event | category | flops | bytes accessed | tf_op | source)
XLA Modules:
  0.0 152.7 jit_solution(19063596596414644)
XLA Ops:
  0.6 1.4 copy.13
  2.0 143.2 %shard_map.119 = (bf16[256,3072]{1,0:T(8,128)(2,1)}, bf16[256,2048]{1,0:T(8,128)(2,1)}, bf16[2,256,1024]{2,1,0:T(8,128)(2,1)}, bf16[2,256,1024]{2,1,0:T(8,128)(2,1)}, bf16[128,3072]{1,0:T(8,128)(2,1)}) custom-call(bf16[256,2048]{1,0:T(8,128)(2,1)} %bitcast.12, bf16[256,1024]{1,0:T(8,128)(2,1)} %bitcast.13, bf16[256,1024]{1,0:T(8,128)(2,1)} %bitcast.14, ...), custom_call_target="tpu_custom_call" | custom-call | flops 27000000512 | bytes 20000000 | tf_op jit(solution)/shard_map/pallas_call | solution.py:526
  145.2 1.9 %add_convert_fusion = bf16[2,256,1024]{2,1,0:T(8,128)(2,1)S(1)} fusion(bf16[2,256,1024]{2,1,0:T(8,128)(2,1)} %get-tuple-element.13, bf16[2,256,1024]{2,1,0:T(8,128)(2,1)} %get-tuple-element.12), kind=kLoop, calls=%fused_computation | loop fusion | flops 2097152 | bytes 3145728 | tf_op jit(solution)/shard_map/convert_element_type | solution.py:590
  147.2 0.0 copy-start.2
  147.2 1.0 fusion
  148.2 0.0 copy-start
  148.2 0.4 copy-done.2
  148.6 1.3 convert_multiply_fusion
  150.0 0.0 copy-done
  150.0 0.0 copy-start.1
  150.0 1.1 copy.16
  151.1 0.6 copy-done.1
  151.8 1.0 copy.17
Async XLA Ops:
  147.2 1.5 copy-start.2
  148.2 1.8 %copy-start = (bf16[256,3072]{1,0:T(8,128)(2,1)S(1)}, bf16[256,3072]{1,0:T(8,128)(2,1)}, u32[]{:S(2)}) copy-start(bf16[256,3072]{1,0:T(8,128)(2,1)} %get-tuple-element.10) | copy-start | bytes 4718596
  150.0 1.8 %copy-start.1 = (bf16[256,2048]{1,0:T(8,128)(2,1)S(1)}, bf16[256,2048]{1,0:T(8,128)(2,1)}, u32[]{:S(2)}) copy-start(bf16[256,2048]{1,0:T(8,128)(2,1)} %get-tuple-element.11) | copy-start | bytes 3145732

commit v6 on v5

--- a/solution.py
+++ b/solution.py
@@ -146,7 +146,7 @@
 
 def layer_kernel(
     q_ref, k_ref, v_ref, list_ref, cnt_ref, len_ref, w_ref, d_ref,
-    lo_ref, dq_ref, gkv_ref, gkv_z_ref, gb_ref,
+    lo_ref, dq_ref, gk_ref, gv_ref, gk_z_ref, gv_z_ref, gb_ref,
     band, raw, lb, wb, db, qs, ds, bias, pb, rb, aa, an, gt, back, gw, rs, rx, gsum,
     local, kv_send, kv_recv, w_send, w_recv, q_recv, pair_send, pair_recv, first_send, l_recv, d_recv,
     a_send, a_recv, row_send, row_recv, z_send, z_recv, rs_send, rs_recv, g_send, g_recv,
@@ -263,9 +263,12 @@
         spread(y_far, j, 0, 512, a_send.at[7], other)
 
     diagonal = lax.broadcasted_iota(jnp.int32, (32, 32), 0) == lax.broadcasted_iota(jnp.int32, (32, 32), 1)
-    used = jnp.max(jnp.where(diagonal, cnt_ref[...], 0), axis=1, keepdims=True)
-    raw[sp] = jnp.full((32, 128), -100, jnp.int32)
-    raw[sp, :, 0:8] = jnp.where(lax.broadcasted_iota(jnp.int32, (32, 8), 1) < used, list_ref[...], -100)
+    slot_of = lax.broadcasted_iota(jnp.int32, (32, 128), 1)
+    listed = jnp.full((32, 128), -100, jnp.int32)
+    for i in range(8):
+        row = jnp.where(cnt_ref[...] > i, list_ref[i : i + 1, :], -100)
+        listed = jnp.where(slot_of == i, jnp.max(jnp.where(diagonal, row, -100), axis=1, keepdims=True), listed)
+    raw[sp] = listed
 
     for copy in loads[:3]:
         copy.wait()
@@ -273,6 +276,7 @@
         weight_quarter(sp, q_recv.at[sp], dp, sp_at(z, x + dx))
     first, *others = chunks(z + 1)
     kv_up(first).start()
+    kv_rows(order[0], True)
     weight_z(sp)
     for j in others:
         kv_up(j).start()
@@ -296,7 +300,6 @@
 
     for dx in (1, 3, 2):
         weight_quarter_here(sp_at(z, x + dx))
-    kv_rows(order[0], True)
     kv_rows(order[1], True)
     kv_here(0, order[0])
     kv_rows(order[0], False)
@@ -334,20 +337,23 @@
 
     def backward(c, _):
         backward_heads(c, qs, band, pb, rb, aa, gt, dp)
+        cols = lanes_of(c, SIZE)
+        for k in (2, 1, 3):
+            remote(
+                band.at[:, 4 - k, :, cols], back.at[k - 1, :, :, cols], row_send.at[k - 1], row_recv.at[k - 1, c], dp, sp_at(z, x - k)
+            ).start()
         return 0
 
-    def backward_chunk(j):
+    def backward_chunk(j, between=None):
         cols = lanes_of(j, 256)
         for k in range(4):
             remote(band.at[:, 0, :, cols], band.at[:, 0, :, cols], kv_send.at[k, j], kv_send.at[k, j], dp, up).wait_send()
-        lax.fori_loop(2 * j, 2 * j + 2, backward, 0)
-
-    def give_back(j):
-        cols = lanes_of(j, 256)
-        for k in (2, 1, 3):
-            remote(
-                band.at[:, 4 - k, :, cols], back.at[k - 1, :, :, cols], row_send.at[k - 1], row_recv.at[k - 1, j], dp, sp_at(z, x - k)
-            ).start()
+        if between is None:
+            lax.fori_loop(2 * j, 2 * j + 2, backward, 0)
+        else:
+            lax.fori_loop(2 * j, 2 * j + 1, backward, 0)
+            between()
+            lax.fori_loop(2 * j + 1, 2 * j + 2, backward, 0)
 
     def spread_in(j):
         for r in range(4):
@@ -374,21 +380,29 @@
 
     own_row, row_above, row_below, row_far = order
 
+    def scatter(j):
+        spread_in(j)
+        weight_grad(j)
+        if j is not own_row:
+            scatter_z(j)
+
     kv_chunk(own_row)
     forward_chunk(own_row)
-    kv_here(0, order[3])
-    kv_rows(order[3], False)
+    kv_here(0, row_far)
+    kv_rows(row_far, False)
+    backward_chunk(own_row)
     weight_relay(0, True)
-    weight_relay(1, True)
     weight_relay(0, False)
-    weight_relay(1, False)
-    backward_chunk(own_row)
-    weight_relay(3, True)
-    weight_relay(3, False)
-    spread_on(own_row)
 
     kv_chunk(row_above)
     forward_chunk(row_above)
+    for dx in (1, 3):
+        weight_relay(dx, True)
+        weight_relay(dx, False)
+    spread_on(own_row)
+
+    kv_chunk(row_below)
+    forward_chunk(row_below)
     weight_relay(2, True)
     weight_pair(row_above)
     weight_relay(2, False)
@@ -397,54 +411,35 @@
     backward_chunk(row_above)
     spread_on(row_above)
     spread_far(own_row)
-
-    kv_chunk(row_below)
-    give_back(own_row)
-    forward_chunk(row_below)
     grad_attn(row_below)
     backward_chunk(row_below)
     spread_on(row_below)
     spread_far(row_above)
     arrived(db.at[pl.ds(0, 7)], d_recv)
-    spread_in(own_row)
-    weight_grad(own_row)
+    scatter(own_row)
+    scatter(row_above)
     for i in range(4):
         weight_here(4 * row_far + i)
     weight_pair(row_far)
 
     kv_chunk(row_far)
-    give_back(row_above)
-    give_back(row_below)
     forward_chunk(row_far)
+    spread_far(row_below)
     grad_attn(row_far)
-    backward_chunk(row_far)
-    give_back(row_far)
+    scatter(row_below)
+    backward_chunk(row_far, lambda: spread_on(row_far))
     dq_out = pltpu.make_async_copy(qs, dq_ref, local.at[7])
     dq_out.start()
-    spread_on(row_far)
-    spread_far(row_below)
-    spread_in(row_above)
-    weight_grad(row_above)
-    scatter_z(row_above)
     spread_far(row_far)
-    spread_in(row_below)
-    weight_grad(row_below)
-    scatter_z(row_below)
-    spread_in(row_far)
-    weight_grad(row_far)
-    scatter_z(row_far)
+    scatter(row_far)
+
     keep = [jnp.where(x + k < 4, 1.0, 0.0).astype(F32) for k in (1, 2, 3)]
 
-    def z_copy(j):
-        cols = lanes_of(j, 256)
-        return remote(band.at[:, 0, :, cols], gkv_z_ref.at[:, :, cols], z_send, z_recv, dp, down)
-
     def row_sums(j):
-        for k in range(3):
-            arrived(back.at[k, :, :, lanes_of(j, 256)], row_recv.at[k, j])
-
         def one(c, _):
             cols = lanes_of(c, SIZE)
+            for k in range(3):
+                arrived(back.at[k, :, :, cols], row_recv.at[k, c])
             below = band[:, 0, :, cols].astype(F32)
             here = band[:, 4, :, cols].astype(F32)
             for k in range(3):
@@ -453,10 +448,11 @@
                 below = below + got * (1.0 - keep[k])
             band[:, 0, :, cols] = below.astype(BF)
             band[:, 4, :, cols] = here.astype(BF)
+            for i in range(2):
+                remote(band.at[i, 0, :, cols], (gk_z_ref, gv_z_ref)[i].at[:, cols], z_send, z_recv, dp, down).start()
             return 0
 
         lax.fori_loop(2 * j, 2 * j + 2, one, 0)
-        z_copy(j).start()
 
     def project(i, _):
         cols = lanes_of(i, 512)
@@ -486,23 +482,36 @@
 
     lax.fori_loop(0, 4, z_sums, 0)
     row_sums(row_above)
+    row_sums(row_below)
     arrived(rx, rs_recv.at[1])
     total = rs[12 + x].astype(F32)
     for r in range(3):
         total = total + rx[r].astype(F32)
     gsum[...] = total.astype(BF)
     g_out = Sends(g_send)
-    for r in range(1, 8):
-        g_out.go(gsum, gb_ref.at[:, lanes_of(dp, PART)], g_recv, (dp + r) % 8, sp)
+
+    def g_block(e):
+        return gb_ref.at[:, lanes_of(e, PART)]
+
+    for to in (y_far, y_up, y_down, other):
+        g_out.go(gsum, g_block(dp), g_recv.at[dp], to, sp)
     own_sum = pltpu.make_async_copy(gsum, gb_ref.at[:, lanes_of(dp, PART)], local.at[9])
     own_sum.start()
 
-    row_sums(row_below)
     row_sums(row_far)
-    arrived(gkv_z_ref, z_recv)
-    gkv_out = pltpu.make_async_copy(band.at[:, 4], gkv_ref, local.at[10])
-    gkv_out.start()
-
+    kv_outs = [
+        pltpu.make_async_copy(band.at[0, 4], gk_ref, local.at[10]),
+        pltpu.make_async_copy(band.at[1, 4], gv_ref, local.at[2]),
+    ]
+    for copy in kv_outs:
+        copy.start()
+    for slot in (y_up, y_down, y_far):
+        arrived(g_block(slot), g_recv.at[slot])
+        g_out.go(g_block(slot), g_block(slot), g_recv.at[slot], other, sp)
+    for r in range(4):
+        slot = dp_at(y + r, 1 - core)
+        arrived(g_block(slot), g_recv.at[slot])
+    arrived(band.at[:, 0], z_recv)
     first_out.finish()
     w_out.finish()
     some = wb.at[:, :, half]
@@ -512,12 +521,11 @@
         remote(some, some, a_send.at[i], a_send.at[i], other, sp).wait_send()
     for k in range(3):
         remote(back.at[k], back.at[k], row_send.at[k], row_send.at[k], dp, up).wait_send()
-    remote(gkv_z_ref, gkv_z_ref, z_send, z_send, dp, down).wait_send()
+    remote(band.at[:, 0], band.at[:, 0], z_send, z_send, dp, down).wait_send()
     remote(rs.at[pl.ds(0, 12)], rs.at[pl.ds(0, 12)], rs_send.at[0], rs_send.at[0], dp, up).wait_send()
     remote(rx, rx, rs_send.at[1], rs_send.at[1], dp, up).wait_send()
-    arrived(gb_ref.at[:, pl.ds(0, 7 * PART)], g_recv)
     g_out.finish()
-    for copy in (dq_out, lo_out, own_sum, gkv_out):
+    for copy in (dq_out, lo_out, own_sum, *kv_outs):
         copy.wait()
 
 
@@ -529,12 +537,14 @@
         + [pl.BlockSpec(memory_space=vmem)] * 2
         + [pl.BlockSpec(memory_space=pltpu.SMEM)]
         + [ANY] * 2,
-        out_specs=[ANY] * 5,
+        out_specs=[ANY] * 7,
         out_shape=[
             jax.ShapeDtypeStruct((TOK, 3072), BF),
             jax.ShapeDtypeStruct((TOK, 2048), BF),
-            jax.ShapeDtypeStruct((2, TOK, 1024), BF),
-            jax.ShapeDtypeStruct((2, TOK, 1024), BF),
+            jax.ShapeDtypeStruct((TOK, 1024), BF),
+            jax.ShapeDtypeStruct((TOK, 1024), BF),
+            jax.ShapeDtypeStruct((TOK, 1024), BF),
+            jax.ShapeDtypeStruct((TOK, 1024), BF),
             jax.ShapeDtypeStruct((128, 3072), BF),
         ],
         scratch_shapes=[
@@ -570,13 +580,13 @@
             DMA((8,)),
             DMA((8, 4)),
             DMA((3,)),
-            DMA((3, 4)),
+            DMA((3, 8)),
             DMA,
             DMA,
             DMA((2,)),
             DMA((2,)),
             DMA((7,)),
-            DMA,
+            DMA((8,)),
         ],
         compiler_params=pltpu.CompilerParams(collective_id=0, has_side_effects=True, vmem_limit_bytes=60 * 2**20),
         cost_estimate=pl.CostEstimate(flops=27 * 10**9, bytes_accessed=20 * 10**6, transcendentals=6 * 10**6),
@@ -584,14 +594,15 @@
 
 
 def per_device(queries, keys, values, key_blocks, block_counts, doc_lengths, out_weight, d_out):
-    layer_out, grad_q, grad_kv, more_kv, grad_all = call_layer(
-        queries[0], keys[0], values[0], key_blocks[0, 0], block_counts[0], doc_lengths, out_weight, d_out[0]
+    layer_out, grad_q, grad_k, grad_v, more_k, more_v, grad_all = call_layer(
+        queries[0], keys[0], values[0], key_blocks[0, 0].T, block_counts[0], doc_lengths, out_weight, d_out[0]
     )
-    grad_kv = (grad_kv.astype(F32) + more_kv.astype(F32)).astype(BF)
+    grad_k = (grad_k.astype(F32) + more_k.astype(F32)).astype(BF)
+    grad_v = (grad_v.astype(F32) + more_v.astype(F32)).astype(BF)
     grad_weight = grad_all.astype(F32)
     tokens = lax.axis_size("dp") * lax.axis_size("sp") * TOK
     grad_weight = grad_weight * (1.0 / math.sqrt(tokens))
-    return (layer_out[None], grad_q[None], grad_kv[:1], grad_kv[1:], grad_weight)
+    return (layer_out[None], grad_q[None], grad_k[None], grad_v[None], grad_weight)
 
 
 def solution(mesh):

time: 155 us -> 147 us (0.948); the launches traced: 153 us -> 147 us
  Pallas kernels: 143 us -> 138 us
  local copies, waits for them, and re-layouts: 5.61 us -> 3.42 us
    pallas_call x1, Pallas kernels: 143 us -> 138 us  [call_layer(): pl.pallas_call(layer_kernel, in_specs=[ANY] * 3 + [pl.BlockSpec(memory_sp...]
    broadcast_in_dim x0 -> x1, other arithmetic: none -> 2.96 us  [per_device(): grad_k[None]]
    convert_element_type x1 -> x0, other arithmetic: 1.93 us -> none  [per_device(): grad_kv = (grad_kv.astype(F32) + more_kv.astype(F32)).astype(BF)]
    unnamed x9 -> x8, local copies, waits for them, and re-layouts: 4.58 us -> 3.42 us
where the time goes in v6:
time: 147 us
  Pallas kernels  138 us (94%)
  other arithmetic  4.28 us (3%)
  local copies, waits for them, and re-layouts  3.42 us (2%)
    pallas_call x1, Pallas kernels, call_layer(): pl.pallas_call(layer_kernel, in_specs=[ANY] * 3 + [pl.BlockSpec(memory_sp...  138 us
    unnamed x8, local copies, waits for them, and re-layouts  3.42 us
    broadcast_in_dim x1, other arithmetic, per_device(): grad_k[None]  2.96 us

profile of v6, /device:TPU:1, one launch (start us, length us, event | category | flops | bytes accessed | tf_op | source)
XLA Modules:
  0.0 146.5 jit_solution(2063712365867935193)
XLA Ops:
  0.6 138.2 %shard_map.119 = (bf16[256,3072]{1,0:T(8,128)(2,1)}, bf16[256,2048]{1,0:T(8,128)(2,1)}, bf16[256,1024]{1,0:T(8,128)(2,1)}, bf16[256,1024]{1,0:T(8,128)(2,1)}, bf...) custom-call(bf16[256,2048]{1,0:T(8,128)(2,1)} %bitcast.17, ...), custom_call_target="tpu_custom_call" | custom-call | flops 27000000512 | bytes 20000000 | tf_op jit(solution)/shard_map/pallas_call | solution.py:534
  138.8 0.0 copy-start.2
  138.8 3.0 %fusion = (bf16[1,256,1024]{2,1,0:T(8,128)(2,1)}, bf16[1,256,1024]{2,1,0:T(8,128)(2,1)}) fusion(bf16[256,1024]{1,0:T(8,128)(2,1)} %get-tuple-element.15, bf16[256,1024]{1,0:T(8,128)(2,1)} %get-tuple-element.14, bf16[256,1024]{1,0:T(8,128)(2,1)} %get-tuple-element.17, bf16[256,1024]{1,0:T(8,128)(2,1)} %get-tuple-element.16), kind=kLoop, calls=%fused_computation.3 | loop fusion | flops 2097152 | bytes 3145728 | tf_op jit(solution)/shard_map/broadcast_in_dim | solution.py:605
  141.8 0.0 copy-start
  141.8 0.0 copy-done.2
  141.8 1.3 convert_multiply_fusion
  143.1 0.7 copy-done
  143.8 0.0 copy-start.1
  143.8 1.1 copy.15
  144.9 0.6 copy-done.1
  145.6 1.0 copy.16
Async XLA Ops:
  138.8 3.0 %copy-start.2 = (bf16[128,3072]{1,0:T(8,128)(2,1)S(1)}, bf16[128,3072]{1,0:T(8,128)(2,1)}, u32[]{:S(2)}) copy-start(bf16[128,3072]{1,0:T(8,128)(2,1)} %get-tuple-element.18) | copy-start | bytes 2359300
  141.8 2.0 %copy-start = (bf16[256,3072]{1,0:T(8,128)(2,1)S(1)}, bf16[256,3072]{1,0:T(8,128)(2,1)}, u32[]{:S(2)}) copy-start(bf16[256,3072]{1,0:T(8,128)(2,1)} %get-tuple-element.12) | copy-start | bytes 4718596
  143.8 1.8 %copy-start.1 = (bf16[256,2048]{1,0:T(8,128)(2,1)S(1)}, bf16[256,2048]{1,0:T(8,128)(2,1)}, u32[]{:S(2)}) copy-start(bf16[256,2048]{1,0:T(8,128)(2,1)} %get-tuple-element.13) | copy-start | bytes 3145732

commit v7 on v6

--- a/solution.py
+++ b/solution.py
@@ -246,9 +246,9 @@
     def spread_here(slot, j):
         arrived(aa.at[slot, pl.ds(j * 512, 512)], a_recv.at[slot, j])
 
-    def spread_own(j):
+    def spread_own(c):
         for i, to in enumerate((y_up, y_down, other)):
-            spread(dp, j, 0, 512, a_send.at[i], to)
+            spread(dp, c // 2, c % 2 * 256, 256, a_send.at[i], to)
 
     def spread_on(j):
         spread_here(y_down, j)
@@ -333,6 +333,7 @@
 
     def forward(c, _):
         forward_heads(c, qs, band, lb, bias, pb, rb, aa, an, dp)
+        spread_own(c)
         return 0
 
     def backward(c, _):
@@ -376,7 +377,6 @@
 
     def forward_chunk(j):
         lax.fori_loop(2 * j, 2 * j + 2, forward, 0)
-        spread_own(j)
 
     own_row, row_above, row_below, row_far = order
 
@@ -415,15 +415,15 @@
     backward_chunk(row_below)
     spread_on(row_below)
     spread_far(row_above)
+    for i in range(4):
+        weight_here(4 * row_far + i)
+    weight_pair(row_far)
+
+    kv_chunk(row_far)
+    forward_chunk(row_far)
     arrived(db.at[pl.ds(0, 7)], d_recv)
     scatter(own_row)
     scatter(row_above)
-    for i in range(4):
-        weight_here(4 * row_far + i)
-    weight_pair(row_far)
-
-    kv_chunk(row_far)
-    forward_chunk(row_far)
     spread_far(row_below)
     grad_attn(row_far)
     scatter(row_below)

time: 147 us -> 145 us (0.986)
  no operation moved by 1% of the time
where the time goes in v7:
time: 145 us
  Pallas kernels  137 us (94%)
  other arithmetic  4.28 us (3%)
  local copies, waits for them, and re-layouts  3.42 us (2%)
    pallas_call x1, Pallas kernels, call_layer(): pl.pallas_call(layer_kernel, in_specs=[ANY] * 3 + [pl.BlockSpec(memory_sp...  137 us
    unnamed x8, local copies, waits for them, and re-layouts  3.42 us
    broadcast_in_dim x1, other arithmetic, per_device(): grad_k[None]  2.96 us

profile of v7, /device:TPU:1, one launch (start us, length us, event | category | flops | bytes accessed | tf_op | source)
XLA Modules:
  0.0 145.1 jit_solution(6152361240825352335)
XLA Ops:
  0.6 136.7 %shard_map.119 = (bf16[256,3072]{1,0:T(8,128)(2,1)}, bf16[256,2048]{1,0:T(8,128)(2,1)}, bf16[256,1024]{1,0:T(8,128)(2,1)}, bf16[256,1024]{1,0:T(8,128)(2,1)}, bf...) custom-call(bf16[256,2048]{1,0:T(8,128)(2,1)} %bitcast.17, ...), custom_call_target="tpu_custom_call" | custom-call | flops 27000000512 | bytes 20000000 | tf_op jit(solution)/shard_map/pallas_call | solution.py:534
  137.4 0.0 copy-start.2
  137.4 3.0 %fusion = (bf16[1,256,1024]{2,1,0:T(8,128)(2,1)}, bf16[1,256,1024]{2,1,0:T(8,128)(2,1)}) fusion(bf16[256,1024]{1,0:T(8,128)(2,1)} %get-tuple-element.15, bf16[256,1024]{1,0:T(8,128)(2,1)} %get-tuple-element.14, bf16[256,1024]{1,0:T(8,128)(2,1)} %get-tuple-element.17, bf16[256,1024]{1,0:T(8,128)(2,1)} %get-tuple-element.16), kind=kLoop, calls=%fused_computation.3 | loop fusion | flops 2097152 | bytes 3145728 | tf_op jit(solution)/shard_map/broadcast_in_dim | solution.py:605
  140.3 0.0 copy-start
  140.3 0.0 copy-done.2
  140.3 1.3 convert_multiply_fusion
  141.6 0.7 copy-done
  142.3 0.0 copy-start.1
  142.3 1.1 copy.15
  143.4 0.6 copy-done.1
  144.1 1.0 copy.16
Async XLA Ops:
  137.4 3.0 %copy-start.2 = (bf16[128,3072]{1,0:T(8,128)(2,1)S(1)}, bf16[128,3072]{1,0:T(8,128)(2,1)}, u32[]{:S(2)}) copy-start(bf16[128,3072]{1,0:T(8,128)(2,1)} %get-tuple-element.18) | copy-start | bytes 2359300
  140.3 2.0 %copy-start = (bf16[256,3072]{1,0:T(8,128)(2,1)S(1)}, bf16[256,3072]{1,0:T(8,128)(2,1)}, u32[]{:S(2)}) copy-start(bf16[256,3072]{1,0:T(8,128)(2,1)} %get-tuple-element.12) | copy-start | bytes 4718596
  142.3 1.8 %copy-start.1 = (bf16[256,2048]{1,0:T(8,128)(2,1)S(1)}, bf16[256,2048]{1,0:T(8,128)(2,1)}, u32[]{:S(2)}) copy-start(bf16[256,2048]{1,0:T(8,128)(2,1)} %get-tuple-element.13) | copy-start | bytes 3145732

commit v8 on v7

--- a/solution.py
+++ b/solution.py
@@ -146,7 +146,7 @@
 
 def layer_kernel(
     q_ref, k_ref, v_ref, list_ref, cnt_ref, len_ref, w_ref, d_ref,
-    lo_ref, dq_ref, gk_ref, gv_ref, gk_z_ref, gv_z_ref, gb_ref,
+    lo_ref, dq_ref, gk_ref, gv_ref, gb_ref,
     band, raw, lb, wb, db, qs, ds, bias, pb, rb, aa, an, gt, back, gw, rs, rx, gsum,
     local, kv_send, kv_recv, w_send, w_recv, q_recv, pair_send, pair_recv, first_send, l_recv, d_recv,
     a_send, a_recv, row_send, row_recv, z_send, z_recv, rs_send, rs_recv, g_send, g_recv,
@@ -448,8 +448,7 @@
                 below = below + got * (1.0 - keep[k])
             band[:, 0, :, cols] = below.astype(BF)
             band[:, 4, :, cols] = here.astype(BF)
-            for i in range(2):
-                remote(band.at[i, 0, :, cols], (gk_z_ref, gv_z_ref)[i].at[:, cols], z_send, z_recv, dp, down).start()
+            remote(band.at[:, 0, :, cols], back.at[3, :, :, cols], z_send, z_recv.at[c], dp, down).start()
             return 0
 
         lax.fori_loop(2 * j, 2 * j + 2, one, 0)
@@ -499,6 +498,15 @@
     own_sum.start()
 
     row_sums(row_far)
+
+    def last(c, _):
+        cols = lanes_of(c, SIZE)
+        arrived(back.at[3, :, :, cols], z_recv.at[c])
+        band[:, 4, :, cols] = (band[:, 4, :, cols].astype(F32) + back[3, :, :, cols].astype(F32)).astype(BF)
+        return 0
+
+    for j in order:
+        lax.fori_loop(2 * j, 2 * j + 2, last, 0)
     kv_outs = [
         pltpu.make_async_copy(band.at[0, 4], gk_ref, local.at[10]),
         pltpu.make_async_copy(band.at[1, 4], gv_ref, local.at[2]),
@@ -511,7 +519,6 @@
     for r in range(4):
         slot = dp_at(y + r, 1 - core)
         arrived(g_block(slot), g_recv.at[slot])
-    arrived(band.at[:, 0], z_recv)
     first_out.finish()
     w_out.finish()
     some = wb.at[:, :, half]
@@ -537,12 +544,10 @@
         + [pl.BlockSpec(memory_space=vmem)] * 2
         + [pl.BlockSpec(memory_space=pltpu.SMEM)]
         + [ANY] * 2,
-        out_specs=[ANY] * 7,
+        out_specs=[ANY] * 5,
         out_shape=[
             jax.ShapeDtypeStruct((TOK, 3072), BF),
             jax.ShapeDtypeStruct((TOK, 2048), BF),
-            jax.ShapeDtypeStruct((TOK, 1024), BF),
-            jax.ShapeDtypeStruct((TOK, 1024), BF),
             jax.ShapeDtypeStruct((TOK, 1024), BF),
             jax.ShapeDtypeStruct((TOK, 1024), BF),
             jax.ShapeDtypeStruct((128, 3072), BF),
@@ -561,7 +566,7 @@
             vmem((8, 2048, TOK), BF),
             vmem((TOK, 2048), BF),
             vmem((2048, TOK), BF),
-            vmem((3, 2, TOK, 1024), BF),
+            vmem((4, 2, TOK, 1024), BF),
             vmem((16, 128, PART), BF),
             vmem((16, 128, PART), BF),
             vmem((3, 128, PART), BF),
@@ -582,7 +587,7 @@
             DMA((3,)),
             DMA((3, 8)),
             DMA,
-            DMA,
+            DMA((8,)),
             DMA((2,)),
             DMA((2,)),
             DMA((7,)),
@@ -594,11 +599,9 @@
 
 
 def per_device(queries, keys, values, key_blocks, block_counts, doc_lengths, out_weight, d_out):
-    layer_out, grad_q, grad_k, grad_v, more_k, more_v, grad_all = call_layer(
+    layer_out, grad_q, grad_k, grad_v, grad_all = call_layer(
         queries[0], keys[0], values[0], key_blocks[0, 0].T, block_counts[0], doc_lengths, out_weight, d_out[0]
     )
-    grad_k = (grad_k.astype(F32) + more_k.astype(F32)).astype(BF)
-    grad_v = (grad_v.astype(F32) + more_v.astype(F32)).astype(BF)
     grad_weight = grad_all.astype(F32)
     tokens = lax.axis_size("dp") * lax.axis_size("sp") * TOK
     grad_weight = grad_weight * (1.0 / math.sqrt(tokens))

time: 145 us -> 147 us (1.014)
  Pallas kernels: 137 us -> 139 us
  other arithmetic: 4.28 us -> 2.56 us
    broadcast_in_dim x1 -> x0, other arithmetic: 2.96 us -> none  [per_device(): grad_k[None]]
    pallas_call x1, Pallas kernels: 137 us -> 139 us  [call_layer(): pl.pallas_call(layer_kernel, in_specs=[ANY] * 3 + [pl.BlockSpec(memory_sp...]
    unnamed x8 -> x12, local copies, waits for them, and re-layouts: 3.42 us -> 4.76 us
where the time goes in v8:
time: 147 us
  Pallas kernels  139 us (95%)
  local copies, waits for them, and re-layouts  4.76 us (3%)
  other arithmetic  2.56 us (2%)
    pallas_call x1, Pallas kernels, call_layer(): pl.pallas_call(layer_kernel, in_specs=[ANY] * 3 + [pl.BlockSpec(memory_sp...  139 us
    unnamed x12, local copies, waits for them, and re-layouts  4.76 us

profile of v8, /device:TPU:1, one launch (start us, length us, event | category | flops | bytes accessed | tf_op | source)
XLA Modules:
  0.0 146.7 jit_solution(2112777101048601797)
XLA Ops:
  0.6 138.7 %shard_map.119 = (bf16[256,3072]{1,0:T(8,128)(2,1)}, bf16[256,2048]{1,0:T(8,128)(2,1)}, bf16[256,1024]{1,0:T(8,128)(2,1)}, bf16[256,1024]{1,0:T(8,128)(2,1)}, bf16[128,3072]{1,0:T(8,128)(2,1)}) custom-call(bf16[256,2048]{1,0:T(8,128)(2,1)} %bitcast.17, bf16[256,1024]{1,0:T(8,128)(2,1)} %bitcast.18, bf16[256,1024]{1,0:T(8,128)(2,1)} %bitcast.19, ...), custom_call_target="tpu_custom_call" | custom-call | flops 27000000512 | bytes 20000000 | tf_op jit(solution)/shard_map/pallas_call | solution.py:541
  139.4 0.0 copy-start
  139.4 2.6 %convert_multiply_fusion = f32[128,3072]{1,0:T(8,128)} fusion(bf16[128,3072]{1,0:T(8,128)(2,1)} %get-tuple-element.14), kind=kLoop, calls=%fused_computation | loop fusion | flops 786432 | bytes 2359296 | tf_op jit(solution)/shard_map/mul | solution.py:607
  141.9 0.0 copy-done
  141.9 0.0 copy-start.1
  141.9 1.1 copy.17
  143.1 0.6 copy-done.1
  143.7 0.0 copy-start.3
  143.7 0.0 copy-start.2
  143.7 1.0 copy.18
  144.7 0.4 copy-done.3
  145.1 0.8 copy.19
  145.9 0.0 copy-done.2
  145.9 0.8 copy.20
Async XLA Ops:
  139.4 2.6 %copy-start = (bf16[256,3072]{1,0:T(8,128)(2,1)S(1)}, bf16[256,3072]{1,0:T(8,128)(2,1)}, u32[]{:S(2)}) copy-start(bf16[256,3072]{1,0:T(8,128)(2,1)} %get-tuple-element.10) | copy-start | bytes 4718596
  141.9 1.8 %copy-start.1 = (bf16[256,2048]{1,0:T(8,128)(2,1)S(1)}, bf16[256,2048]{1,0:T(8,128)(2,1)}, u32[]{:S(2)}) copy-start(bf16[256,2048]{1,0:T(8,128)(2,1)} %get-tuple-element.11) | copy-start | bytes 3145732
  143.7 1.4 copy-start.3
  143.7 2.2 %copy-start.2 = (bf16[256,1024]{1,0:T(8,128)(2,1)S(1)}, bf16[256,1024]{1,0:T(8,128)(2,1)}, u32[]{:S(2)}) copy-start(bf16[256,1024]{1,0:T(8,128)(2,1)} %get-tuple-element.13) | copy-start | bytes 1572868
